TPU v7x, 32 devices: a whole 2x2x4 slice. The times are simulated.
32 devices in a mesh: section: 8 (over z, x), band: 4 (over y, core).
Axes of the slice: x: 2, y: 2, z: 4, core: 2. Of those that a mesh axis runs over, the one named last changes fastest.
Arguments:
- echoes: bfloat16 [2, 4096, 2, 16384], P(None, ('band', 'section')), may hold values from -6 to 6
- replica: float32 [2, 2048], replicated, may hold values from -0.09375 to 0.09375
- azimuth_taps: float32 [256, 2, 1024], P(('section', 'band')), may hold values from -0.125 to 0.125
- coefficients: bfloat16 [256, 8, 64, 128], P(('section', 'band')), may hold values from -2 to 2
- offsets: int32 [256, 128], P(('section', 'band')), may hold values from 0 to 57
- block_order: int32 [2], replicated, may hold values from 0 to 1, each once
Outputs:
- image: bfloat16 [2, 16384, 2, 4096], P(None, ('section', 'band'))
Inputs may be any that keep to these rules, and one draw needn't show every extreme that they name: `block_order`: each block appears once.
All inputs are finite; a program needn't handle non-finite values.
Results may differ from a plain program's by a relative error of at most 0.015.
Values may be sent and summed in bfloat16 or wider, within the bound.
A program may use at most 256 MiB of HBM per device.

v0:
```python
import math

import jax
import jax.numpy as jnp
from jax import lax
from jax.sharding import PartitionSpec as P

RANGE_BINS = 16384
PULSES = 4096
FACTOR = 128
BAND_BINS = 64
MARGIN_BINS = 32
KERNEL = 8
BLOCKS = 2


def extended(cells, sides, width):
    for axis, dim in sides:
        count = lax.axis_size(axis)
        ends = count - 1
        head = lax.slice_in_dim(cells, 0, width, axis=dim)
        tail = lax.slice_in_dim(cells, cells.shape[dim] - width, cells.shape[dim], axis=dim)
        cells = jnp.concatenate(
            [
                lax.ppermute(tail, axis, [(i, (i + 1) % count) for i in range(ends)]),
                cells,
                lax.ppermute(head, axis, [((i + 1) % count, i) for i in range(ends)]),
            ],
            axis=dim,
        )
    return cells


def phases(outer_size, inner_size, length):
    outer_index = jnp.arange(outer_size, dtype=jnp.int32)[:, None]
    inner_index = jnp.arange(inner_size, dtype=jnp.int32)[None, :]
    return 2.0 * math.pi / length * (outer_index * inner_index % length).astype(jnp.float32)


def left_matrix(phase_table, signum):
    cosine = jnp.cos(phase_table)
    sine_part = signum * jnp.sin(phase_table)
    upper_rows = jnp.stack([cosine, -sine_part], axis=1)
    lower_rows = jnp.stack([sine_part, cosine], axis=1)
    return jnp.stack([upper_rows, lower_rows], axis=0)


def right_matrix(phase_table, signum):
    cosine = jnp.cos(phase_table)
    sine_part = signum * jnp.sin(phase_table)
    leading = jnp.stack([cosine, sine_part], axis=1)
    trailing = jnp.stack([-sine_part, cosine], axis=1)
    return jnp.stack([leading, trailing], axis=0)


def rotate_by(real_part, imag_part, phase_table, signum):
    cosine = jnp.cos(phase_table)
    sine_part = signum * jnp.sin(phase_table)
    return (real_part * cosine - imag_part * sine_part, real_part * sine_part + imag_part * cosine)


def make_tables(length):
    outer_size = length // FACTOR
    outer_phase = phases(outer_size, outer_size, outer_size)
    inner_phase = phases(FACTOR, FACTOR, FACTOR)
    twist_phase = phases(outer_size, FACTOR, length)
    return (
        left_matrix(outer_phase, -1.0).astype(jnp.bfloat16),
        right_matrix(inner_phase, -1.0).astype(jnp.bfloat16),
        twist_phase,
        left_matrix(outer_phase, 1.0).astype(jnp.bfloat16),
        right_matrix(inner_phase, 1.0).astype(jnp.bfloat16),
    )


def contract(pattern, left_side, right_side):
    return jnp.einsum(pattern, left_side, right_side, preferred_element_type=jnp.float32)


def exact_spectrum(tap_rows, length):
    outer_size = length // FACTOR
    padded = jnp.pad(tap_rows, ((0, 0), (0, 0), (0, length - tap_rows.shape[2])))
    padded = padded.reshape(tap_rows.shape[0], 2, outer_size, FACTOR)
    outer_phase = phases(outer_size, outer_size, outer_size)
    inner_phase = phases(FACTOR, FACTOR, FACTOR)
    twist_phase = phases(outer_size, FACTOR, length)
    mixed_rows = jnp.einsum(
        "ckdn,bdnm->bckm", left_matrix(outer_phase, -1.0), padded, precision=lax.Precision.HIGHEST
    )
    real_part, imag_part = rotate_by(mixed_rows[:, 0], mixed_rows[:, 1], twist_phase, -1.0)
    rotated = jnp.stack([real_part, imag_part], axis=1)
    return jnp.einsum(
        "bdkn,dnem->bkem", rotated, right_matrix(inner_phase, -1.0), precision=lax.Precision.HIGHEST
    )


def matched(values, spectrum):
    real_part = values[..., 0, :]
    imag_part = values[..., 1, :]
    spec_real = spectrum[..., 0, :]
    spec_imag = spectrum[..., 1, :]
    return jnp.stack(
        [
            real_part * spec_real + imag_part * spec_imag,
            imag_part * spec_real - real_part * spec_imag,
        ],
        axis=-2,
    ).astype(jnp.bfloat16)


def compress_range(signal, spectrum, tables):
    pulse_rows = signal.shape[0]
    outer_size = RANGE_BINS // FACTOR
    mixed_rows = contract(
        "ckdn,bdnm->bckm", tables[0], signal.reshape(pulse_rows, 2, outer_size, FACTOR)
    )
    real_part, imag_part = rotate_by(mixed_rows[:, 0], mixed_rows[:, 1], tables[2], -1.0)
    rotated = jnp.stack([real_part, imag_part], axis=1).astype(jnp.bfloat16)
    spectral = contract("bdkn,dnem->bkem", rotated, tables[1])
    filtered = matched(spectral, spectrum)
    returned = contract("bkdn,dnem->bkem", filtered, tables[4])
    real_part, imag_part = rotate_by(returned[:, :, 0], returned[:, :, 1], tables[2], 1.0)
    turned = jnp.stack([real_part, imag_part], axis=1).astype(jnp.bfloat16)
    lines = (contract("cmek,bekq->bcmq", tables[3], turned) * (1.0 / RANGE_BINS)).astype(
        jnp.bfloat16
    )
    return lines.reshape(pulse_rows, 2, RANGE_BINS)


def build_migration(coefficients, offsets):
    columns = jnp.arange(BAND_BINS + 2 * MARGIN_BINS, dtype=jnp.int32)[None, None, :, None]
    targets = (
        jnp.arange(BAND_BINS, dtype=jnp.int32)[None, :, None, None] + offsets[:, None, None, :]
    )
    migration_table = jnp.zeros(
        (coefficients.shape[0], BAND_BINS, BAND_BINS + 2 * MARGIN_BINS, coefficients.shape[3]),
        jnp.float32,
    )
    for tap_index in range(KERNEL):
        weights = coefficients[:, tap_index, :, None, :].astype(jnp.float32)
        migration_table = migration_table + jnp.where(
            columns == targets + tap_index, weights, jnp.zeros((), jnp.float32)
        )
    return migration_table.astype(jnp.bfloat16)


def migrate(padded, migration_table):
    range_rows = padded.shape[3] - 2 * MARGIN_BINS
    band_count = range_rows // BAND_BINS
    lead = padded.shape[:3]
    head_rows = padded[..., :range_rows].reshape(lead + (band_count, BAND_BINS))
    tail_rows = padded[..., BAND_BINS : BAND_BINS + range_rows].reshape(
        lead + (band_count, BAND_BINS)
    )
    window = jnp.concatenate([head_rows, tail_rows], axis=4)
    shifted = contract("jitg,kcgjt->kcgji", migration_table, window)
    return shifted.reshape(lead + (range_rows,))


def focus_azimuth(turned, migration_table, band_spectra, tables):
    range_rows = turned.shape[2]
    outer_size = PULSES // FACTOR
    signal = turned.reshape(outer_size, FACTOR, 2, range_rows)
    mixed_rows = contract("ckdn,nmdr->kmcr", tables[0], signal)
    twist = tables[2][:, :, None]
    real_part, imag_part = rotate_by(mixed_rows[:, :, 0], mixed_rows[:, :, 1], twist, -1.0)
    rotated = jnp.stack([real_part, imag_part], axis=2).astype(jnp.bfloat16)
    spectral = contract("kndr,dnem->kemr", rotated, tables[1]).astype(jnp.bfloat16)
    padded = extended(spectral, ((("section", "band"), 3),), MARGIN_BINS)
    moved = migrate(padded, migration_table)
    real_part = moved[:, 0]
    imag_part = moved[:, 1]
    spec_real = band_spectra[:, 0]
    spec_imag = band_spectra[:, 1]
    filtered = jnp.stack(
        [
            real_part * spec_real + imag_part * spec_imag,
            imag_part * spec_real - real_part * spec_imag,
        ],
        axis=1,
    ).astype(jnp.bfloat16)
    returned = contract("kdnr,dnem->kemr", filtered, tables[4])
    real_part, imag_part = rotate_by(returned[:, 0], returned[:, 1], twist, 1.0)
    back = jnp.stack([real_part, imag_part], axis=1).astype(jnp.bfloat16)
    focused = (contract("cmek,keqr->rcmq", tables[3], back) * (1.0 / PULSES)).astype(jnp.bfloat16)
    return focused.reshape(range_rows, 2, PULSES)


def corner_turn(compressed):
    pulse_rows = compressed.shape[0]
    block_count = compressed.shape[1]
    sections = lax.axis_size("section")
    band_count = lax.axis_size("band")
    local_rows = RANGE_BINS // (sections * band_count)
    shaped = compressed.reshape(1, 1, pulse_rows, block_count, 2, sections, band_count, local_rows)
    across_bands = lax.all_to_all(shaped, "band", split_axis=6, concat_axis=0, tiled=True)
    across_sections = lax.all_to_all(
        across_bands, "section", split_axis=5, concat_axis=1, tiled=True
    )
    arrived = across_sections.reshape(
        band_count * sections * pulse_rows, block_count, 2, local_rows
    )
    return arrived


def on_device(echoes, replica, azimuth_taps, coefficients, offsets, block_order):
    range_tables = make_tables(RANGE_BINS)
    pulse_tables = make_tables(PULSES)
    range_spectrum = exact_spectrum(replica[None], RANGE_BINS)[0]
    spectra = exact_spectrum(azimuth_taps, PULSES)
    band_spectra = jnp.repeat(jnp.transpose(spectra, (1, 2, 3, 0)), BAND_BINS, axis=3)
    migration_table = build_migration(coefficients, offsets)
    images = []
    for position in range(BLOCKS):
        signal = lax.dynamic_index_in_dim(echoes, block_order[position], 0, keepdims=False)
        compressed = compress_range(signal, range_spectrum, range_tables)
        turned = corner_turn(compressed[:, None])
        images.append(focus_azimuth(turned[:, 0], migration_table, band_spectra, pulse_tables))
    return jnp.stack(images, axis=0)


def solution(mesh):
    in_specs = (
        P(None, ("band", "section"), None, None),
        P(),
        P(("section", "band"), None, None),
        P(("section", "band"), None, None, None),
        P(("section", "band"), None),
        P(),
    )
    out_specs = P(None, ("section", "band"), None, None)
    return jax.shard_map(
        on_device, mesh=mesh, in_specs=in_specs, out_specs=out_specs, check_vma=False
    )
```

profile of v0, /device:TPU:24, one launch (start us, length us, event | category | flops | bytes accessed | tf_op | source)
XLA Modules:
  0.0 1844.5 jit_solution(1695525299507660108)
XLA Ops:
  6.8 15.0 constant_dynamic-slice_fusion.1
  21.8 21.1 %copy.334 = bf16[1,128,2,16384]{1,3,2,0:T(8,128)(2,1)} copy(bf16[1,128,2,16384]{3,2,1,0:T(2,128)(2,1)} %get-tuple-element.34) | data formatting | bytes 16777216
  43.0 13.5 copy.283
  56.5 21.1 %copy.329 = bf16[1,128,2,16384]{1,3,2,0:T(8,128)(2,1)} copy(bf16[1,128,2,16384]{3,2,1,0:T(2,128)(2,1)} %get-tuple-element.33) | data formatting | bytes 16777216
  77.6 13.4 copy.258
  105.6 14.9 subtract_convert_fusion.11
  125.4 12.0 convolution_bitcast_fusion.4
  137.4 15.2 add_convert_fusion.11
  152.7 11.8 fusion.52
  172.0 16.1 subtract_convert_fusion.9
  192.7 13.6 copy.237
  226.5 13.5 copy.195
  247.8 65.0 %all-to-all-done.2 = bf16[1,1,128,1,2,8,4,512]{2,7,5,4,3,1,0,6:T(8,128)(2,1)} async-done(((bf16[1,1,128,1,2,8,4,512]{2,7,5,4,3,1,0,6:T(8,128)(2,1)}), bf16[1,1,128,1,2,8,4,512]{2,7,5,4,3,1,0,6:T(8,128)(2,1)}, u32[]{:S(2)}, u32[]{:S(2)}) %all-to-all-start.2) | async-done | bytes 8388640 | tf_op jit(solution)/shard_map/all_to_all | solution.py:196
  326.3 85.5 %all-to-all-done = bf16[1,1,128,1,2,8,4,512]{2,7,5,4,3,1,0,6:T(8,128)(2,1)} async-done(((bf16[1,1,128,1,2,8,4,512]{2,7,5,4,3,1,0,6:T(8,128)(2,1)}), bf16[1,1,128,1,2,8,4,512]{2,7,5,4,3,1,0,6:T(8,128)(2,1)}, u32[]{:S(2)}, u32[]{:S(2)}) %all-to-all-start) | async-done | bytes 8388640 | tf_op jit(solution)/shard_map/all_to_all | solution.py:196
  425.5 173.6 %all-to-all-done.3 = bf16[4,1,128,1,2,8,1,512]{2,7,0,4,6,3,1,5:T(8,128)(2,1)} async-done(((bf16[4,1,128,1,2,8,1,512]{2,7,0,4,6,3,1,5:T(8,128)(2,1)}), bf16[4,1,128,1,2,8,1,512]{2,7,0,4,6,3,1,5:T(8,128)(2,1)}, u32[]{:S(2)}, u32[]{:S(2)}) %all-to-all-start.3) | async-done | bytes 8388640 | tf_op jit(solution)/shard_map/all_to_all | solution.py:197
  648.0 14.7 copy.240
  662.7 10.8 convolution_bitcast_fusion
  673.4 112.9 %all-to-all-done.1 = bf16[4,1,128,1,2,8,1,512]{2,7,0,4,6,3,1,5:T(8,128)(2,1)} async-done(((bf16[4,1,128,1,2,8,1,512]{2,7,0,4,6,3,1,5:T(8,128)(2,1)}), bf16[4,1,128,1,2,8,1,512]{2,7,0,4,6,3,1,5:T(8,128)(2,1)}, u32[]{:S(2)}, u32[]{:S(2)}) %all-to-all-start.1) | async-done | bytes 8388640 | tf_op jit(solution)/shard_map/all_to_all | solution.py:197
  786.4 14.7 copy.198
  801.0 12.9 convolution_bitcast_fusion.3
  814.1 12.5 subtract_convert_fusion.8
  833.1 13.6 fusion.20
  871.0 13.6 fusion.19
  905.6 17.7 pad_maximum_fusion.2
  923.3 11.9 copy.245
  935.2 24.0 %copy.249 = bf16[32,2,128,8,64]{4,0,1,3,2:T(8,128)(2,1)} copy(bf16[32,2,128,8,64]{2,4,3,1,0:T(8,128)(2,1)} %bitcast.393) | data formatting | bytes 16777216 | tf_op jit(solution)/shard_map/reshape | solution.py:151
  959.3 11.9 copy.248
  971.2 24.1 %copy.250 = bf16[32,2,128,8,64]{4,0,1,3,2:T(8,128)(2,1)} copy(bf16[32,2,128,8,64]{2,4,3,1,0:T(8,128)(2,1)} %bitcast.394) | data formatting | bytes 16777216 | tf_op jit(solution)/shard_map/reshape | solution.py:152
  995.4 231.2 %fusion.13 = f32[32,2,128,8,64]{4,0,1,3,2:T(8,128)} fusion(bf16[32,2,128,8,64]{4,0,1,3,2:T(8,128)(2,1)} %copy.250, bf16[32,2,128,8,64]{4,0,1,3,2:T(8,128)(2,1)} %copy.249, f32[8,64,128]{1,0,2:T(8,128)} %copy.219, s32[8,64,128]{1,0,2:T(8,128)} %get-tuple-element.74, f32[8,64,128]{1,0,2:T(8,128)} %copy.218, s32[8,64,128]{1,0,2:T(8,128)} %get-tuple-element.75, ...), kind=kOutput, calls=%fused_computation.29 | convolution fusion | flops 1308622848 | bytes 37748736 | tf_op jit(solution)/shard_map/jitg,kcgjt->kcgji/dot_general | solution.py:77
  1226.7 27.6 %copy.251 = f32[32,2,128,8,64]{2,4,3,1,0:T(8,128)} copy(f32[32,2,128,8,64]{4,0,1,3,2:T(8,128)} %fusion.13) | data formatting | bytes 33554432 | tf_op jit(solution)/shard_map/jitg,kcgjt->kcgji/transpose | solution.py:77
  1254.2 11.2 fusion.181
  1288.1 18.2 pad_maximum_fusion.4
  1306.3 12.0 copy.205
  1318.3 24.0 %copy.209 = bf16[32,2,128,8,64]{4,0,1,3,2:T(8,128)(2,1)} copy(bf16[32,2,128,8,64]{2,4,3,1,0:T(8,128)(2,1)} %bitcast.395) | data formatting | bytes 16777216 | tf_op jit(solution)/shard_map/reshape | solution.py:151
  1342.4 12.0 copy.208
  1354.4 24.1 %copy.210 = bf16[32,2,128,8,64]{4,0,1,3,2:T(8,128)(2,1)} copy(bf16[32,2,128,8,64]{2,4,3,1,0:T(8,128)(2,1)} %bitcast.396) | data formatting | bytes 16777216 | tf_op jit(solution)/shard_map/reshape | solution.py:152
  1378.5 231.2 %fusion.16 = f32[32,2,128,8,64]{4,0,1,3,2:T(8,128)} fusion(bf16[32,2,128,8,64]{4,0,1,3,2:T(8,128)(2,1)} %copy.210, bf16[32,2,128,8,64]{4,0,1,3,2:T(8,128)(2,1)} %copy.209, f32[8,64,128]{1,0,2:T(8,128)} %copy.219, s32[8,64,128]{1,0,2:T(8,128)} %get-tuple-element.74, f32[8,64,128]{1,0,2:T(8,128)} %copy.218, s32[8,64,128]{1,0,2:T(8,128)} %get-tuple-element.75, ...), kind=kOutput, calls=%fused_computation.30 | convolution fusion | flops 1308622848 | bytes 37748736 | tf_op jit(solution)/shard_map/jitg,kcgjt->kcgji/dot_general | solution.py:77
  1609.7 27.6 %copy.220 = f32[32,2,128,8,64]{2,4,3,1,0:T(8,128)} copy(f32[32,2,128,8,64]{4,0,1,3,2:T(8,128)} %fusion.16) | data formatting | bytes 33554432 | tf_op jit(solution)/shard_map/jitg,kcgjt->kcgji/transpose | solution.py:77
  1637.3 11.1 fusion.179
  1666.5 22.5 %add_convert_fusion.8 = (bf16[32,1,128,512]{3,2,1,0:T(8,128)(2,1)S(1)}, bf16[32,1,128,512]{3,2,1,0:T(8,128)(2,1)}, bf16[32,1,128,512]{3,2,1,0:T(8,128)(2,1)}, bf16[32,1,128,512]{3,2,1,0:T(8,128)(2,1)}) fusion(f32[32,1,128,512]{3,2,1,0:T(8,128)} %copy.332, f32[32,1,128,512]{3,2,1,0:T(8,128)} %copy.333, f32[32,1,128,512]{3,2,1,0:T(8,128)} %copy.330, ...), kind=kLoop, calls=%fused_computation.104 | loop fusion | flops 33554432 | bytes 67108864 | tf_op jit(solution)/shard_map/convert.30
  1694.0 10.7 fusion.53
  1704.8 12.0 subtract_convert_fusion.6
  1724.5 17.5 fusion.60
  1741.9 11.5 copy.229
  1759.8 17.5 fusion.64
  1777.3 11.5 copy.256
  1788.8 13.8 pad_maximum_fusion
  1802.6 41.5 %copy.257 = bf16[2,512,2,4096]{3,2,1,0:T(2,128)(2,1)} copy(bf16[2,512,2,4096]{1,3,2,0:T(8,128)(2,1)} %pad_maximum_fusion) | data formatting | bytes 33554432 | tf_op jit(solution)/shard_map/stack | solution.py:219
  (149 shorter events, 250.1 us)
Async XLA Ops:
  91.1 5.0 slice-start
  91.1 5.9 slice-start.1
  97.0 7.5 copy-start.25
  137.4 27.0 %copy-start.6 = (bf16[1,128,2,128]{3,1,2,0:T(8,128)(2,1)}, bf16[1,128,2,128]{3,1,2,0:T(8,128)(2,1)S(1)}, u32[]{:S(2)}) copy-start(bf16[1,128,2,128]{3,1,2,0:T(8,128)(2,1)S(1)} %get-tuple-element.82) | copy-start | bytes 196612
  137.4 27.0 %copy-start.8 = (bf16[1,128,2,128]{3,1,2,0:T(8,128)(2,1)}, bf16[1,128,2,128]{3,1,2,0:T(8,128)(2,1)S(1)}, u32[]{:S(2)}) copy-start(bf16[1,128,2,128]{3,1,2,0:T(8,128)(2,1)S(1)} %get-tuple-element.89) | copy-start | bytes 196612
  152.7 11.8 copy-start.3
  152.7 11.8 copy-start.4
  214.0 98.8 %all-to-all-start.2 = ((bf16[1,1,128,1,2,8,4,512]{2,7,5,4,3,1,0,6:T(8,128)(2,1)}), bf16[1,1,128,1,2,8,4,512]{2,7,5,4,3,1,0,6:T(8,128)(2,1)}, u32[]{:S(2)}, u32[]{:S(2)}) async-start(bf16[1,1,128,1,2,8,4,512]{2,7,5,4,3,1,0,6:T(8,128)(2,1)} %copy.238), calls=%async_computation.2 | async-start | bytes 16777216 | tf_op jit(solution)/shard_map/all_to_all | solution.py:196
  312.7 99.0 %all-to-all-start = ((bf16[1,1,128,1,2,8,4,512]{2,7,5,4,3,1,0,6:T(8,128)(2,1)}), bf16[1,1,128,1,2,8,4,512]{2,7,5,4,3,1,0,6:T(8,128)(2,1)}, u32[]{:S(2)}, u32[]{:S(2)}) async-start(bf16[1,1,128,1,2,8,4,512]{2,7,5,4,3,1,0,6:T(8,128)(2,1)} %copy.196), calls=%async_computation | async-start | bytes 16777216 | tf_op jit(solution)/shard_map/all_to_all | solution.py:196
  411.7 187.4 %all-to-all-start.3 = ((bf16[4,1,128,1,2,8,1,512]{2,7,0,4,6,3,1,5:T(8,128)(2,1)}), bf16[4,1,128,1,2,8,1,512]{2,7,0,4,6,3,1,5:T(8,128)(2,1)}, u32[]{:S(2)}, u32[]{:S(2)}) async-start(bf16[4,1,128,1,2,8,1,512]{2,7,0,4,6,3,1,5:T(8,128)(2,1)} %copy.239), calls=%async_computation.3 | async-start | bytes 16777216 | tf_op jit(solution)/shard_map/all_to_all | solution.py:197
  425.5 180.8 %copy-start.28 = (s32[8,128]{1,0:T(8,128)S(1)}, s32[8,128]{1,0:T(8,128)}, u32[]{:S(2)}) copy-start(s32[8,128]{1,0:T(8,128)} %param.10) | copy-start | bytes 12292
  425.5 181.5 %copy-start.5 = (bf16[8,8,64,128]{3,2,1,0:T(8,128)(2,1)S(1)}, bf16[8,8,64,128]{3,2,1,0:T(8,128)(2,1)}, u32[]{:S(2)}) copy-start(bf16[8,8,64,128]{3,2,1,0:T(8,128)(2,1)} %param.9) | copy-start | bytes 3145732
  599.2 187.2 %all-to-all-start.1 = ((bf16[4,1,128,1,2,8,1,512]{2,7,0,4,6,3,1,5:T(8,128)(2,1)}), bf16[4,1,128,1,2,8,1,512]{2,7,0,4,6,3,1,5:T(8,128)(2,1)}, u32[]{:S(2)}, u32[]{:S(2)}) async-start(bf16[4,1,128,1,2,8,1,512]{2,7,0,4,6,3,1,5:T(8,128)(2,1)} %copy.197), calls=%async_computation.1 | async-start | bytes 16777216 | tf_op jit(solution)/shard_map/all_to_all | solution.py:197
  605.7 0.6 copy-start.23
  605.7 13.9 copy-start.21
  635.1 10.5 copy-start.20
  801.0 13.1 copy-start
  846.7 3.3 copy-start.2
  854.3 47.6 %collective-permute-start.2 = (bf16[32,2,128,32]{2,3,1,0:T(8,128)(2,1)S(1)}, bf16[32,2,128,32]{2,3,1,0:T(8,128)(2,1)S(1)}, u32[]{:S(2)}, u32[]{:S(2)}) collective-permute-start(bf16[32,2,128,32]{2,3,1,0:T(8,128)(2,1)S(1)} %copy.243), channel_id=1, source_target_pairs={{0,1},{1,2},{2,3},{3,4},{4,5},{5,6},{6,7},{7,8},{8,9},{9,10},{10,1... | collective-permute-start | bytes 1572872 | tf_op jit(solution)/shard_map/ppermute | solution.py:25
  857.7 45.2 %collective-permute-start.3 = (bf16[32,2,128,32]{2,3,1,0:T(8,128)(2,1)}, bf16[32,2,128,32]{2,3,1,0:T(8,128)(2,1)}, u32[]{:S(2)}, u32[]{:S(2)}) collective-permute-start(bf16[32,2,128,32]{2,3,1,0:T(8,128)(2,1)} %copy.246), channel_id=1, source_target_pairs={{1,0},{2,1},{3,2},{4,3},{5,4},{6,5},{7,6},{8,7},{9,8},{10,9},{11,1... | collective-permute-start | bytes 1572872 | tf_op jit(solution)/shard_map/ppermute | solution.py:27
  884.7 3.2 copy-start.1
  893.0 390.5 %collective-permute-start = (bf16[32,2,128,32]{2,3,1,0:T(8,128)(2,1)}, bf16[32,2,128,32]{2,3,1,0:T(8,128)(2,1)}, u32[]{:S(2)}, u32[]{:S(2)}) collective-permute-start(bf16[32,2,128,32]{2,3,1,0:T(8,128)(2,1)} %copy.203), channel_id=1, source_target_pairs={{0,1},{1,2},{2,3},{3,4},{4,5},{5,6},{6,7},{7,8},{8,9},{9,10},{10,1... | collective-permute-start | bytes 1572872 | tf_op jit(solution)/shard_map/ppermute | solution.py:25
  896.5 389.0 %collective-permute-start.1 = (bf16[32,2,128,32]{2,3,1,0:T(8,128)(2,1)}, bf16[32,2,128,32]{2,3,1,0:T(8,128)(2,1)}, u32[]{:S(2)}, u32[]{:S(2)}) collective-permute-start(bf16[32,2,128,32]{2,3,1,0:T(8,128)(2,1)} %copy.206), channel_id=1, source_target_pairs={{1,0},{2,1},{3,2},{4,3},{5,4},{6,5},{7,6},{8,7},{9,8},{10,9},{11,1... | collective-permute-start | bytes 1572872 | tf_op jit(solution)/shard_map/ppermute | solution.py:27
  971.2 24.2 %copy-start.10 = (f32[8,64,128]{1,0,2:T(8,128)S(1)}, f32[8,64,128]{1,0,2:T(8,128)}, u32[]{:S(2)}) copy-start(f32[8,64,128]{1,0,2:T(8,128)} %copy.212) | copy-start | bytes 786436
  971.2 24.2 %copy-start.11 = (f32[8,64,128]{1,0,2:T(8,128)S(1)}, f32[8,64,128]{1,0,2:T(8,128)}, u32[]{:S(2)}) copy-start(f32[8,64,128]{1,0,2:T(8,128)} %copy.213) | copy-start | bytes 786436
  971.2 24.2 %copy-start.12 = (f32[8,64,128]{1,0,2:T(8,128)S(1)}, f32[8,64,128]{1,0,2:T(8,128)}, u32[]{:S(2)}) copy-start(f32[8,64,128]{1,0,2:T(8,128)} %copy.214) | copy-start | bytes 786436
  971.2 24.2 %copy-start.14 = (f32[8,64,128]{1,0,2:T(8,128)S(1)}, f32[8,64,128]{1,0,2:T(8,128)}, u32[]{:S(2)}) copy-start(f32[8,64,128]{1,0,2:T(8,128)} %copy.215) | copy-start | bytes 786436
  971.2 24.2 %copy-start.16 = (f32[8,64,128]{1,0,2:T(8,128)S(1)}, f32[8,64,128]{1,0,2:T(8,128)}, u32[]{:S(2)}) copy-start(f32[8,64,128]{1,0,2:T(8,128)} %copy.216) | copy-start | bytes 786436
  971.2 24.2 %copy-start.18 = (f32[8,64,128]{1,0,2:T(8,128)S(1)}, f32[8,64,128]{1,0,2:T(8,128)}, u32[]{:S(2)}) copy-start(f32[8,64,128]{1,0,2:T(8,128)} %copy.217) | copy-start | bytes 786436
  1354.3 24.2 %copy-start.13 = (f32[8,64,128]{1,0,2:T(8,128)S(1)}, f32[8,64,128]{1,0,2:T(8,128)}, u32[]{:S(2)}) copy-start(f32[8,64,128]{1,0,2:T(8,128)} %copy.214) | copy-start | bytes 786436
  1354.4 24.2 %copy-start.15 = (f32[8,64,128]{1,0,2:T(8,128)S(1)}, f32[8,64,128]{1,0,2:T(8,128)}, u32[]{:S(2)}) copy-start(f32[8,64,128]{1,0,2:T(8,128)} %copy.215) | copy-start | bytes 786436
  1354.4 24.2 %copy-start.17 = (f32[8,64,128]{1,0,2:T(8,128)S(1)}, f32[8,64,128]{1,0,2:T(8,128)}, u32[]{:S(2)}) copy-start(f32[8,64,128]{1,0,2:T(8,128)} %copy.216) | copy-start | bytes 786436
  1354.4 24.2 %copy-start.19 = (f32[8,64,128]{1,0,2:T(8,128)S(1)}, f32[8,64,128]{1,0,2:T(8,128)}, u32[]{:S(2)}) copy-start(f32[8,64,128]{1,0,2:T(8,128)} %copy.217) | copy-start | bytes 786436
  1666.5 22.5 %copy-start.7 = (bf16[1,128,2,128]{3,1,2,0:T(8,128)(2,1)S(1)}, bf16[1,128,2,128]{3,1,2,0:T(8,128)(2,1)}, u32[]{:S(2)}) copy-start(bf16[1,128,2,128]{3,1,2,0:T(8,128)(2,1)} %copy-done.6) | copy-start | bytes 196612
  1666.5 22.5 %copy-start.9 = (bf16[1,128,2,128]{3,1,2,0:T(8,128)(2,1)S(1)}, bf16[1,128,2,128]{3,1,2,0:T(8,128)(2,1)}, u32[]{:S(2)}) copy-start(bf16[1,128,2,128]{3,1,2,0:T(8,128)(2,1)} %copy-done.8) | copy-start | bytes 196612
  1694.0 10.8 copy-start.22
  1694.0 10.7 copy-start.24
  1716.8 7.6 copy-start.26
  1716.8 7.7 copy-start.27
where the time goes:
time: 1860 us; the launch traced here: 1840 us
  matrix products  626 us (34%)
  local copies, waits for them, and re-layouts  560 us (30%)
  waiting for transfers between devices  437 us (23%)
  other arithmetic  178 us (10%)
  starting transfers between devices  38.7 us (2%)
    dot_general x18, matrix products, contract(): jnp.einsum(pattern, left_side, right_side, preferred_element_type=jnp.flo...  624 us
    all_to_all x2, waiting for transfers between devices, corner_turn(): lax.all_to_all(across_bands, 'section', split_axis=5, concat_axis=1, tile...  287 us
    all_to_all x2, waiting for transfers between devices, corner_turn(): lax.all_to_all(shaped, 'band', split_axis=6, concat_axis=0, tiled=True)  150 us
    unnamed x72, local copies, waits for them, and re-layouts  105 us
    another operation x10, other arithmetic  93.9 us
    transpose x2, local copies, waits for them, and re-layouts, contract(): jnp.einsum(pattern, left_side, right_side, preferred_element_type=jnp.flo...  55.2 us
    reshape x2, local copies, waits for them, and re-layouts, migrate(): padded[..., BAND_BINS:BAND_BINS + range_rows]  48.3 us
    reshape x2, local copies, waits for them, and re-layouts, migrate(): head_rows = padded[..., :range_rows].reshape(lead + (band_count, BAND_BINS))  48.1 us
  transfers between devices with their start and end apart: 8, of which 4 were waited for; matrix products, arithmetic and copies ran while one was open for 28% of the time, Pallas kernels for 0%

commit v1 on v0

--- a/solution.py
+++ b/solution.py
@@ -1,8 +1,11 @@
+import functools
 import math
 
 import jax
 import jax.numpy as jnp
 from jax import lax
+from jax.experimental import pallas as pl
+from jax.experimental.pallas import tpu as pltpu
 from jax.sharding import PartitionSpec as P
 
 RANGE_BINS = 16384
@@ -203,19 +206,235 @@
     return arrived
 
 
+def compress_send_kernel(
+    axes,
+    x_ref,
+    left_ref,
+    right_ref,
+    right_back_ref,
+    left_back_ref,
+    cosine_ref,
+    sine_ref,
+    spec_real_ref,
+    spec_imag_ref,
+    arrived_ref,
+    outbox,
+    send_sem,
+    recv_sem,
+    local_sem,
+):
+    (major, major_size), (minor, minor_size) = axes
+    count = major_size * minor_size
+    step = pl.program_id(0)
+    steps = pl.num_programs(0)
+    pairs = outbox.shape[2]
+    per_block = arrived_ref.shape[2] // pairs
+    block = step // per_block
+    first = (step % per_block) * pairs
+    me = lax.axis_index(major) * minor_size + lax.axis_index(minor)
+    source = lax.axis_index(minor) * major_size + lax.axis_index(major)
+
+    @pl.when(step == 0)
+    def _():
+        barrier = pltpu.get_barrier_semaphore()
+
+        def greet(k, carry):
+            other = (me + k) % count
+            pl.semaphore_signal(
+                barrier,
+                inc=1,
+                device_id={major: other // minor_size, minor: other % minor_size},
+                device_id_type=pl.DeviceIdType.MESH,
+            )
+            return carry
+
+        lax.fori_loop(1, count, greet, 0)
+        pl.semaphore_wait(barrier, count - 1)
+
+    left = left_ref[...]
+    right = right_ref[...]
+    right_back = right_back_ref[...]
+    left_back = left_back_ref[...]
+    half = FACTOR
+
+    def one_pair(pair, carry):
+        cosine = cosine_ref[...]
+        sine = sine_ref[...]
+        spec_real = spec_real_ref[...]
+        spec_imag = spec_imag_ref[...]
+        signal = jnp.concatenate([x_ref[0, 2 * pair], x_ref[0, 2 * pair + 1]], axis=1)
+        mixed = jnp.dot(left, signal, preferred_element_type=jnp.float32)
+        rows = []
+        for p in range(2):
+            lanes = slice(p * half, (p + 1) * half)
+            re, im = mixed[:half, lanes], mixed[half:, lanes]
+            rows.append(
+                jnp.concatenate([re * cosine + im * sine, im * cosine - re * sine], axis=1).astype(
+                    jnp.bfloat16
+                )
+            )
+        spectral = jnp.dot(
+            jnp.concatenate(rows, axis=0), right, preferred_element_type=jnp.float32
+        )
+        rows = []
+        for p in range(2):
+            part = spectral[p * half : (p + 1) * half]
+            re, im = part[:, :half], part[:, half:]
+            rows.append(
+                jnp.concatenate(
+                    [re * spec_real + im * spec_imag, im * spec_real - re * spec_imag], axis=1
+                ).astype(jnp.bfloat16)
+            )
+        returned = jnp.dot(
+            jnp.concatenate(rows, axis=0), right_back, preferred_element_type=jnp.float32
+        )
+        columns = []
+        for p in range(2):
+            part = returned[p * half : (p + 1) * half]
+            re, im = part[:, :half], part[:, half:]
+            columns.append(
+                jnp.concatenate([re * cosine - im * sine, re * sine + im * cosine], axis=0).astype(
+                    jnp.bfloat16
+                )
+            )
+        lines = jnp.dot(
+            left_back, jnp.concatenate(columns, axis=1), preferred_element_type=jnp.float32
+        ) * (1.0 / RANGE_BINS)
+        tile = lines.shape[0] // count
+        packed = jnp.concatenate(
+            [
+                lines[:, :half].reshape(count, tile, half),
+                lines[:, half:].reshape(count, tile, half),
+            ],
+            axis=1,
+        ).astype(jnp.bfloat16)
+        outbox[step, :, pair] = packed
+        return carry
+
+    lax.fori_loop(0, pairs, one_pair, 0)
+
+    own = pltpu.make_async_copy(
+        outbox.at[step, me], arrived_ref.at[block, source, pl.ds(first, pairs)], local_sem
+    )
+    own.start()
+
+    def post(k, carry):
+        other = (me + k * 11) % count
+        pltpu.make_async_remote_copy(
+            src_ref=outbox.at[step, other],
+            dst_ref=arrived_ref.at[block, source, pl.ds(first, pairs)],
+            send_sem=send_sem,
+            recv_sem=recv_sem,
+            device_id={major: other // minor_size, minor: other % minor_size},
+            device_id_type=pl.DeviceIdType.MESH,
+        ).start()
+        return carry
+
+    lax.fori_loop(1, count, post, 0)
+    own.wait()
+
+    @pl.when(step == steps - 1)
+    def _():
+        whole = arrived_ref.at[:, pl.ds(0, count - 1)]
+        pltpu.make_async_copy(whole, whole, send_sem).wait()
+        pltpu.make_async_copy(whole, whole, recv_sem).wait()
+
+
+def compress_and_turn(echoes, spectrum, axes):
+    blocks, pulses, _, length = echoes.shape
+    count = axes[0][1] * axes[1][1]
+    outer_size = length // FACTOR
+    rows_each = outer_size // count
+    chunk = 16
+    signal = (
+        echoes.reshape(blocks, pulses, 2, outer_size, FACTOR)
+        .transpose(0, 1, 3, 2, 4)
+        .reshape(blocks, pulses, 2 * outer_size, FACTOR)
+    )
+    tables = make_tables(length)
+    left = tables[0].transpose(0, 1, 3, 2).reshape(2 * outer_size, 2 * outer_size)
+    right = tables[1].reshape(2 * FACTOR, 2 * FACTOR)
+    right_back = tables[4].reshape(2 * FACTOR, 2 * FACTOR)
+    left_back = (
+        tables[3]
+        .reshape(2, count, rows_each, 2 * outer_size)
+        .transpose(1, 0, 2, 3)
+        .reshape(2 * outer_size, 2 * outer_size)
+    )
+    steps_per_block = pulses // chunk
+    steps = blocks * steps_per_block
+    pairs = chunk // 2
+    tile = 4 * rows_each
+
+    def whole(array):
+        return pl.BlockSpec(array.shape, lambda s: (0,) * array.ndim)
+
+    operands = (
+        left,
+        right,
+        right_back,
+        left_back,
+        jnp.cos(tables[2]),
+        jnp.sin(tables[2]),
+        spectrum[:, 0],
+        spectrum[:, 1],
+    )
+    return pl.pallas_call(
+        functools.partial(compress_send_kernel, axes),
+        grid=(steps,),
+        in_specs=[
+            pl.BlockSpec(
+                (1, chunk, 2 * outer_size, FACTOR),
+                lambda s: (s // steps_per_block, s % steps_per_block, 0, 0),
+            )
+        ]
+        + [whole(array) for array in operands],
+        out_specs=pl.BlockSpec(memory_space=pl.ANY),
+        out_shape=jax.ShapeDtypeStruct(
+            (blocks, count, pulses // 2, tile, FACTOR), jnp.bfloat16
+        ),
+        scratch_shapes=[
+            pltpu.VMEM((steps, count, pairs, tile, FACTOR), jnp.bfloat16),
+            pltpu.SemaphoreType.DMA,
+            pltpu.SemaphoreType.DMA,
+            pltpu.SemaphoreType.DMA,
+        ],
+        compiler_params=pltpu.CompilerParams(
+            collective_id=0, has_side_effects=True, vmem_limit_bytes=44 * 2**20
+        ),
+        cost_estimate=pl.CostEstimate(
+            flops=blocks * pulses * 16 * FACTOR**2 * 2 * FACTOR,
+            bytes_accessed=4 * echoes.size,
+            transcendentals=0,
+        ),
+        name="compress_turn",
+    )(signal, *operands)
+
+
 def on_device(echoes, replica, azimuth_taps, coefficients, offsets, block_order):
+    sections = lax.axis_size("section")
+    bands = lax.axis_size("band")
+    count = sections * bands
+    direct = (RANGE_BINS // FACTOR) == 4 * count and echoes.shape[1] % 16 == 0
     range_tables = make_tables(RANGE_BINS)
     pulse_tables = make_tables(PULSES)
     range_spectrum = exact_spectrum(replica[None], RANGE_BINS)[0]
     spectra = exact_spectrum(azimuth_taps, PULSES)
     band_spectra = jnp.repeat(jnp.transpose(spectra, (1, 2, 3, 0)), BAND_BINS, axis=3)
     migration_table = build_migration(coefficients, offsets)
+    if direct:
+        arrived = compress_and_turn(
+            echoes, range_spectrum, (("section", sections), ("band", bands))
+        ).reshape(echoes.shape[0], PULSES, 2, RANGE_BINS // count)
     images = []
     for position in range(BLOCKS):
-        signal = lax.dynamic_index_in_dim(echoes, block_order[position], 0, keepdims=False)
-        compressed = compress_range(signal, range_spectrum, range_tables)
-        turned = corner_turn(compressed[:, None])
-        images.append(focus_azimuth(turned[:, 0], migration_table, band_spectra, pulse_tables))
+        if direct:
+            turned = lax.dynamic_index_in_dim(arrived, block_order[position], 0, keepdims=False)
+        else:
+            signal = lax.dynamic_index_in_dim(echoes, block_order[position], 0, keepdims=False)
+            compressed = compress_range(signal, range_spectrum, range_tables)
+            turned = corner_turn(compressed[:, None])[:, 0]
+        images.append(focus_azimuth(turned, migration_table, band_spectra, pulse_tables))
     return jnp.stack(images, axis=0)
 
 

time: 1860 us -> 1560 us (0.84)
  waiting for transfers between devices: 437 us -> 0.01 us
  Pallas kernels: 0 us -> 373 us
  local copies, waits for them, and re-layouts: 560 us -> 445 us
  matrix products: 626 us -> 571 us
  other arithmetic: 178 us -> 135 us
  starting transfers between devices: 38.7 us -> 11.5 us
    all_to_all x4 -> x0, waiting for transfers between devices: 437 us -> none  [the longest x2 287 us: corner_turn(): lax.all_to_all(across_bands, 'section', split_axis=5, concat_axis=1, tile...]
    pallas_call x0 -> x1, Pallas kernels: none -> 373 us  [compress_and_turn(): pl.pallas_call(functools.partial(compress_send_kernel, axes), grid=(steps...]
    dot_general x18 -> x10, matrix products: 624 us -> 570 us  [contract(): jnp.einsum(pattern, left_side, right_side, preferred_element_type=jnp.flo...]
    all_to_all x4 -> x0, local copies, waits for them, and re-layouts: 44.8 us -> none  [the longest x2 29.3 us: corner_turn(): lax.all_to_all(across_bands, 'section', split_axis=5, concat_axis=1, tile...]
    another operation x10 -> x8, other arithmetic: 93.9 us -> 52.1 us
    convert_element_type x2, local copies, waits for them, and re-layouts: 27 us -> 0.27 us  [the longest x1 0.14 us: make_tables(): right_matrix(inner_phase, 1.0).astype(jnp.bfloat16)]
    unnamed x72 -> x75, local copies, waits for them, and re-layouts: 105 us -> 79 us
    all_to_all x4 -> x0, starting transfers between devices: 23.9 us -> none  [the longest x2 12.4 us: corner_turn(): lax.all_to_all(across_bands, 'section', split_axis=5, concat_axis=1, tile...]
  transfers between devices with their start and end apart: 8 -> 4, of which waited for: 4 -> 0; matrix products, arithmetic and copies ran while one was open for 28% -> 29% of each run, Pallas kernels for 0% -> 0%
where the time goes in v1:
time: 1560 us; the launch traced here: 1540 us
  matrix products  571 us (37%)
  local copies, waits for them, and re-layouts  445 us (29%)
  Pallas kernels  373 us (24%)
  other arithmetic  135 us (9%)
    dot_general x10, matrix products, contract(): jnp.einsum(pattern, left_side, right_side, preferred_element_type=jnp.flo...  570 us
    pallas_call x1, Pallas kernels, compress_and_turn(): pl.pallas_call(functools.partial(compress_send_kernel, axes), grid=(steps...  373 us
    unnamed x75, local copies, waits for them, and re-layouts  79 us
    transpose x2, local copies, waits for them, and re-layouts, contract(): jnp.einsum(pattern, left_side, right_side, preferred_element_type=jnp.flo...  55.2 us
    another operation x7, other arithmetic  52.1 us
    reshape x2, local copies, waits for them, and re-layouts, migrate(): padded[..., BAND_BINS:BAND_BINS + range_rows]  48.3 us
    reshape x2, local copies, waits for them, and re-layouts, migrate(): head_rows = padded[..., :range_rows].reshape(lead + (band_count, BAND_BINS))  48 us
    another operation x1, local copies, waits for them, and re-layouts, on_device(): return jnp.stack(images, axis=0)  41.5 us
  transfers between devices with their start and end apart: 4, of which 0 were waited for; matrix products, arithmetic and copies ran while one was open for 29% of the time, Pallas kernels for 0%

profile of v1, /device:TPU:24, one launch (start us, length us, event | category | flops | bytes accessed | tf_op | source)
XLA Modules:
  0.0 1540.4 jit_solution(5095643133055813634)
XLA Ops:
  9.9 373.1 %compress_turn.1 = bf16[2,32,64,16,128]{4,3,2,1,0:T(8,128)(2,1)} custom-call(bf16[2,128,256,128]{3,2,1,0:T(8,128)(2,1)} %bitcast.277, bf16[256,256]{1,0:T(8,128)(2,1)S(1)} %copy.173.left_ref, bf16[256,256]{1,0:T(8,128)(2,1)S(1)} %bitcast.260, bf16[256,256]{1,0:T(8,128)(2,1)S(1)} %bitcast.259, bf16[256,256]{1,0:T(8,128)(2,1)S(1)} %reshape.540.left_back_ref, ...), custom_call_target="tpu_custom_call" | custom-call | flops 17179869184 | bytes 33554432 | tf_op jit(solution)/shard_map/compress_turn/pallas_call | solution.py:382
  383.0 24.8 %reshape.543 = bf16[2,4096,2,512]{3,2,1,0:T(2,128)(2,1)} reshape(bf16[2,32,64,16,128]{4,3,2,1,0:T(8,128)(2,1)} %compress_turn.1) | data formatting | bytes 33554432 | tf_op jit(solution)/shard_map/reshape | solution.py:428
  409.2 14.2 constant_dynamic-slice_fusion.1
  423.4 8.0 copy.269
  431.4 8.0 copy.274
  439.5 18.5 %convolution_bitcast_fusion.1 = f32[32,128,2,512]{3,0,2,1:T(8,128)} fusion(bf16[32,128,2,512,1]{3,1,0,2,4:T(8,128)(2,1)} %bitcast.261, f32[1,32,2,32]{3,1,2,0:T(8,128)S(1)} %get-tuple-element.72, f32[1,32,2,32]{3,1,2,0:T(8,128)S(1)} %get-tuple-element.71), kind=kOutput, calls=%fused_computation.28 | convolution fusion | flops 536887296 | bytes 25182208 | tf_op jit(solution)/shard_map/ckdn,nmdr->kmcr/dot_general | solution.py:80
  458.1 10.2 convolution_bitcast_fusion
  468.3 16.3 %subtract_convert_fusion.5 = (bf16[32,128,1,512]{3,0,2,1:T(8,128)(2,1)S(1)}, bf16[32,128,1,512]{3,0,2,1:T(8,128)(2,1)}, bf16[32,128,1,512]{3,0,2,1:T(8,128)(2,1)}, bf16[32,128,1,512]{3,0,2,1:T(8,128)(2,1)}) fusion(f32[32,128,2,512]{3,0,2,1:T(8,128)} %convolution_bitcast_fusion.1, f32[32,128]{0,1:T(8,128)S(1)} %copy.177, f32[32,128]{0,1:T(8,128)S(1)} %copy.176, ...), kind=kLoop, calls=%fused_computation.68 | loop fusion | flops 33554432 | bytes 50364416 | tf_op jit(solution)/shard_map/convert.26
  484.6 6.5 pad_maximum_fusion.5
  491.1 13.6 fusion.17
  519.1 7.6 pad_maximum_fusion.6
  526.7 13.6 fusion.18
  549.1 5.1 collective-permute-start.3
  569.8 6.5 fusion.144
  576.3 9.1 copy.271
  585.3 9.1 copy.273
  602.1 17.4 %pad_maximum_fusion.4 = (bf16[32,2,128,512]{3,2,0,1:T(8,128)(2,1)}, bf16[32,2,128,512]{3,2,0,1:T(8,128)(2,1)}) fusion(bf16[32,2,128,512]{3,2,0,1:T(8,128)(2,1)} %copy-done.2, bf16[32,2,128,32]{3,2,0,1:T(8,128)(2,1)S(1)} %copy.181, bf16[32,2,128,32]{3,2,0,1:T(8,128)(2,1)} %copy.184), kind=kLoop, calls=%fused_computation.34 | loop fusion | flops 33554432 | bytes 26214400 | tf_op jit(solution)/shard_map/concatenate | solution.py:26
  619.5 11.9 copy.182
  631.5 24.0 %copy.186 = bf16[32,2,128,8,64]{4,0,1,3,2:T(8,128)(2,1)} copy(bf16[32,2,128,8,64]{2,4,3,1,0:T(8,128)(2,1)} %bitcast.266) | data formatting | bytes 16777216 | tf_op jit(solution)/shard_map/reshape | solution.py:154
  655.4 11.9 copy.185
  667.4 24.1 %copy.187 = bf16[32,2,128,8,64]{4,0,1,3,2:T(8,128)(2,1)} copy(bf16[32,2,128,8,64]{2,4,3,1,0:T(8,128)(2,1)} %bitcast.267) | data formatting | bytes 16777216 | tf_op jit(solution)/shard_map/reshape | solution.py:155
  691.6 231.2 %fusion.14 = f32[32,2,128,8,64]{4,0,1,3,2:T(8,128)} fusion(bf16[32,2,128,8,64]{4,0,1,3,2:T(8,128)(2,1)} %copy.187, bf16[32,2,128,8,64]{4,0,1,3,2:T(8,128)(2,1)} %copy.186, f32[8,64,128]{1,0,2:T(8,128)} %copy.196, s32[8,64,128]{1,0,2:T(8,128)} %get-tuple-element.56, f32[8,64,128]{1,0,2:T(8,128)} %copy.195, s32[8,64,128]{1,0,2:T(8,128)} %get-tuple-element.57, ...), kind=kOutput, calls=%fused_computation.26 | convolution fusion | flops 1308622848 | bytes 37748736 | tf_op jit(solution)/shard_map/jitg,kcgjt->kcgji/dot_general | solution.py:80
  922.8 27.6 %copy.197 = f32[32,2,128,8,64]{2,4,3,1,0:T(8,128)} copy(f32[32,2,128,8,64]{4,0,1,3,2:T(8,128)} %fusion.14) | data formatting | bytes 33554432 | tf_op jit(solution)/shard_map/jitg,kcgjt->kcgji/transpose | solution.py:80
  950.4 11.2 fusion.143
  961.5 9.0 copy.272
  970.5 9.0 copy.270
  984.2 18.0 %pad_maximum_fusion.2 = (bf16[32,2,128,512]{3,2,0,1:T(8,128)(2,1)}, bf16[32,2,128,512]{3,2,0,1:T(8,128)(2,1)}) fusion(bf16[32,2,128,512]{3,2,0,1:T(8,128)(2,1)} %copy-done.1, bf16[32,2,128,32]{3,2,0,1:T(8,128)(2,1)S(1)} %copy.212, bf16[32,2,128,32]{3,2,0,1:T(8,128)(2,1)} %copy.215), kind=kLoop, calls=%fused_computation.32 | loop fusion | flops 33554432 | bytes 26214400 | tf_op jit(solution)/shard_map/concatenate | solution.py:26
  1002.2 12.0 copy.213
  1014.1 24.0 %copy.217 = bf16[32,2,128,8,64]{4,0,1,3,2:T(8,128)(2,1)} copy(bf16[32,2,128,8,64]{2,4,3,1,0:T(8,128)(2,1)} %bitcast.268) | data formatting | bytes 16777216 | tf_op jit(solution)/shard_map/reshape | solution.py:154
  1038.1 12.0 copy.216
  1050.1 24.1 %copy.218 = bf16[32,2,128,8,64]{4,0,1,3,2:T(8,128)(2,1)} copy(bf16[32,2,128,8,64]{2,4,3,1,0:T(8,128)(2,1)} %bitcast.269) | data formatting | bytes 16777216 | tf_op jit(solution)/shard_map/reshape | solution.py:155
  1074.3 231.2 %fusion.11 = f32[32,2,128,8,64]{4,0,1,3,2:T(8,128)} fusion(bf16[32,2,128,8,64]{4,0,1,3,2:T(8,128)(2,1)} %copy.218, bf16[32,2,128,8,64]{4,0,1,3,2:T(8,128)(2,1)} %copy.217, f32[8,64,128]{1,0,2:T(8,128)} %copy.196, s32[8,64,128]{1,0,2:T(8,128)} %get-tuple-element.56, f32[8,64,128]{1,0,2:T(8,128)} %copy.195, s32[8,64,128]{1,0,2:T(8,128)} %get-tuple-element.57, ...), kind=kOutput, calls=%fused_computation.25 | convolution fusion | flops 1308622848 | bytes 37748736 | tf_op jit(solution)/shard_map/jitg,kcgjt->kcgji/dot_general | solution.py:80
  1305.5 27.6 %copy.219 = f32[32,2,128,8,64]{2,4,3,1,0:T(8,128)} copy(f32[32,2,128,8,64]{4,0,1,3,2:T(8,128)} %fusion.11) | data formatting | bytes 33554432 | tf_op jit(solution)/shard_map/jitg,kcgjt->kcgji/transpose | solution.py:80
  1333.1 11.1 fusion.145
  1344.2 9.1 copy.276
  1353.3 8.9 copy.275
  1362.2 22.4 %add_convert_fusion.5 = (bf16[32,1,128,512]{3,2,1,0:T(8,128)(2,1)}, bf16[32,1,128,512]{3,2,1,0:T(8,128)(2,1)}, bf16[32,1,128,512]{3,2,1,0:T(8,128)(2,1)S(1)}, bf16[32,1,128,512]{3,2,1,0:T(8,128)(2,1)}) fusion(f32[32,1,128,512]{3,2,1,0:T(8,128)} %copy.272, f32[32,1,128,512]{3,2,1,0:T(8,128)} %copy.273, f32[32,1,128,512]{3,2,1,0:T(8,128)} %copy.270, ...), kind=kLoop, calls=%fused_computation.66 | loop fusion | flops 33554432 | bytes 67108864 | tf_op jit(solution)/shard_map/convert.24
  1384.7 5.0 fusion.36
  1389.8 10.7 fusion.35
  1400.5 12.1 subtract_convert_fusion.3
  1412.6 7.6 maximum_bitcast_fusion.2
  1420.2 17.8 %fusion.41 = bf16[512,2,32,128]{0,2,1,3:T(8,128)(2,1)} fusion(bf16[32,2,128,512,1]{3,2,0,1,4:T(8,128)(2,1)} %maximum_bitcast_fusion.2, bf16[1,32,2,32]{3,1,2,0:T(8,128)(2,1)S(1)} %copy-done.29, bf16[1,32,2,32]{3,1,2,0:T(8,128)(2,1)S(1)} %copy-done.28), kind=kOutput, calls=%fused_computation.71 | convolution fusion | flops 545275904 | bytes 16785408 | tf_op jit(solution)/shard_map/cmek,keqr->rcmq/dot_general | solution.py:80
  1438.0 11.4 copy.206
  1449.5 6.3 maximum_bitcast_fusion.5
  1455.8 17.5 %fusion.44 = bf16[512,2,32,128]{0,2,1,3:T(8,128)(2,1)} fusion(bf16[32,2,128,512,1]{3,2,0,1,4:T(8,128)(2,1)} %maximum_bitcast_fusion.5, bf16[1,32,2,32]{3,1,2,0:T(8,128)(2,1)S(1)} %copy-done.29, bf16[1,32,2,32]{3,1,2,0:T(8,128)(2,1)S(1)} %copy-done.28), kind=kOutput, calls=%fused_computation.72 | convolution fusion | flops 545275904 | bytes 16785408 | tf_op jit(solution)/shard_map/cmek,keqr->rcmq/dot_general | solution.py:80
  1473.3 11.5 copy.224
  1484.9 13.8 pad_maximum_fusion
  1498.7 41.5 %copy.225 = bf16[2,512,2,4096]{3,2,1,0:T(2,128)(2,1)} copy(bf16[2,512,2,4096]{1,3,2,0:T(8,128)(2,1)} %pad_maximum_fusion) | data formatting | bytes 33554432 | tf_op jit(solution)/shard_map/stack | solution.py:438
  (139 shorter events, 57.9 us)
Async XLA Ops:
  4.5 1.8 copy-start.23
  4.5 556.8 %copy-start.21 = (f32[32,128]{1,0:T(8,128)}, f32[32,128]{1,0:T(8,128)S(1)}, u32[]{:S(2)}) copy-start(f32[32,128]{1,0:T(8,128)S(1)} %get-tuple-element.88) | copy-start | bytes 49156
  6.9 0.6 copy-start.3
  6.9 0.6 copy-start.5
  439.5 18.6 %copy-start.16 = (f32[1,32,2,32]{3,1,2,0:T(8,128)}, f32[1,32,2,32]{3,1,2,0:T(8,128)S(1)}, u32[]{:S(2)}) copy-start(f32[1,32,2,32]{3,1,2,0:T(8,128)S(1)} %get-tuple-element.71) | copy-start | bytes 24580
  439.5 18.6 %copy-start.18 = (f32[1,32,2,32]{3,1,2,0:T(8,128)}, f32[1,32,2,32]{3,1,2,0:T(8,128)S(1)}, u32[]{:S(2)}) copy-start(f32[1,32,2,32]{3,1,2,0:T(8,128)S(1)} %get-tuple-element.72) | copy-start | bytes 24580
  439.5 18.6 %copy-start = (bf16[1,4096,2,512]{3,1,2,0:T(8,128)(2,1)S(1)}, bf16[1,4096,2,512]{3,1,2,0:T(8,128)(2,1)}, u32[]{:S(2)}) copy-start(bf16[1,4096,2,512]{3,1,2,0:T(8,128)(2,1)} %copy.274) | copy-start | bytes 25165828
  504.7 3.4 copy-start.2
  513.1 86.3 %collective-permute-start.1 = (bf16[32,2,128,32]{2,3,1,0:T(8,128)(2,1)}, bf16[32,2,128,32]{2,3,1,0:T(8,128)(2,1)}, u32[]{:S(2)}, u32[]{:S(2)}) collective-permute-start(bf16[32,2,128,32]{2,3,1,0:T(8,128)(2,1)} %copy.183), channel_id=1, source_target_pairs={{1,0},{2,1},{3,2},{4,3},{5,4},{6,5},{7,6},{8,7},{9,8},{10,9},{11,1... | collective-permute-start | bytes 1572872 | tf_op jit(solution)/shard_map/ppermute | solution.py:30
  516.7 80.8 %collective-permute-start = (bf16[32,2,128,32]{2,3,1,0:T(8,128)(2,1)}, bf16[32,2,128,32]{2,3,1,0:T(8,128)(2,1)}, u32[]{:S(2)}, u32[]{:S(2)}) collective-permute-start(bf16[32,2,128,32]{2,3,1,0:T(8,128)(2,1)} %copy.180), channel_id=1, source_target_pairs={{0,1},{1,2},{2,3},{3,4},{4,5},{5,6},{6,7},{7,8},{8,9},{9,10},{10,1... | collective-permute-start | bytes 1572872 | tf_op jit(solution)/shard_map/ppermute | solution.py:28
  540.4 3.3 copy-start.1
  543.7 15.3 copy-start.30
  543.7 17.2 %copy-start.17 = (f32[1,32,2,32]{3,1,2,0:T(8,128)S(1)}, f32[1,32,2,32]{3,1,2,0:T(8,128)}, u32[]{:S(2)}) copy-start(f32[1,32,2,32]{3,1,2,0:T(8,128)} %copy-done.16) | copy-start | bytes 24580
  543.7 17.2 %copy-start.19 = (f32[1,32,2,32]{3,1,2,0:T(8,128)S(1)}, f32[1,32,2,32]{3,1,2,0:T(8,128)}, u32[]{:S(2)}) copy-start(f32[1,32,2,32]{3,1,2,0:T(8,128)} %copy-done.18) | copy-start | bytes 24580
  543.7 17.6 %copy-start.24 = (f32[32,128]{1,0:T(8,128)S(1)}, f32[32,128]{1,0:T(8,128)}, u32[]{:S(2)}) copy-start(f32[32,128]{1,0:T(8,128)} %copy-done.23) | copy-start | bytes 49156
  543.7 18.2 %copy-start.7 = (bf16[8,8,64,128]{3,2,1,0:T(8,128)(2,1)S(1)}, bf16[8,8,64,128]{3,2,1,0:T(8,128)(2,1)}, u32[]{:S(2)}) copy-start(bf16[8,8,64,128]{3,2,1,0:T(8,128)(2,1)} %param.9) | copy-start | bytes 3145732
  549.1 432.4 %collective-permute-start.3 = (bf16[32,2,128,32]{2,3,1,0:T(8,128)(2,1)}, bf16[32,2,128,32]{2,3,1,0:T(8,128)(2,1)}, u32[]{:S(2)}, u32[]{:S(2)}) collective-permute-start(bf16[32,2,128,32]{2,3,1,0:T(8,128)(2,1)} %copy.214), channel_id=1, source_target_pairs={{1,0},{2,1},{3,2},{4,3},{5,4},{6,5},{7,6},{8,7},{9,8},{10,9},{11,1... | collective-permute-start | bytes 1572872 | tf_op jit(solution)/shard_map/ppermute | solution.py:30
  555.7 423.9 %collective-permute-start.2 = (bf16[32,2,128,32]{2,3,1,0:T(8,128)(2,1)}, bf16[32,2,128,32]{2,3,1,0:T(8,128)(2,1)}, u32[]{:S(2)}, u32[]{:S(2)}) collective-permute-start(bf16[32,2,128,32]{2,3,1,0:T(8,128)(2,1)} %copy.211), channel_id=1, source_target_pairs={{0,1},{1,2},{2,3},{3,4},{4,5},{5,6},{6,7},{7,8},{8,9},{9,10},{10,1... | collective-permute-start | bytes 1572872 | tf_op jit(solution)/shard_map/ppermute | solution.py:28
  585.3 9.2 copy-start.26
  585.3 9.2 copy-start.27
  585.3 9.8 copy-start.20
  667.4 24.2 %copy-start.8 = (f32[8,64,128]{1,0,2:T(8,128)S(1)}, f32[8,64,128]{1,0,2:T(8,128)}, u32[]{:S(2)}) copy-start(f32[8,64,128]{1,0,2:T(8,128)} %copy.193) | copy-start | bytes 786436
  667.4 24.2 %copy-start.10 = (f32[8,64,128]{1,0,2:T(8,128)S(1)}, f32[8,64,128]{1,0,2:T(8,128)}, u32[]{:S(2)}) copy-start(f32[8,64,128]{1,0,2:T(8,128)} %copy.192) | copy-start | bytes 786436
  667.4 24.2 %copy-start.12 = (f32[8,64,128]{1,0,2:T(8,128)S(1)}, f32[8,64,128]{1,0,2:T(8,128)}, u32[]{:S(2)}) copy-start(f32[8,64,128]{1,0,2:T(8,128)} %copy.191) | copy-start | bytes 786436
  667.4 24.2 %copy-start.14 = (f32[8,64,128]{1,0,2:T(8,128)S(1)}, f32[8,64,128]{1,0,2:T(8,128)}, u32[]{:S(2)}) copy-start(f32[8,64,128]{1,0,2:T(8,128)} %copy.190) | copy-start | bytes 786436
  1050.1 24.2 %copy-start.9 = (f32[8,64,128]{1,0,2:T(8,128)S(1)}, f32[8,64,128]{1,0,2:T(8,128)}, u32[]{:S(2)}) copy-start(f32[8,64,128]{1,0,2:T(8,128)} %copy.193) | copy-start | bytes 786436
  1050.1 24.2 %copy-start.11 = (f32[8,64,128]{1,0,2:T(8,128)S(1)}, f32[8,64,128]{1,0,2:T(8,128)}, u32[]{:S(2)}) copy-start(f32[8,64,128]{1,0,2:T(8,128)} %copy.192) | copy-start | bytes 786436
  1050.1 24.2 %copy-start.13 = (f32[8,64,128]{1,0,2:T(8,128)S(1)}, f32[8,64,128]{1,0,2:T(8,128)}, u32[]{:S(2)}) copy-start(f32[8,64,128]{1,0,2:T(8,128)} %copy.191) | copy-start | bytes 786436
  1050.1 24.2 %copy-start.15 = (f32[8,64,128]{1,0,2:T(8,128)S(1)}, f32[8,64,128]{1,0,2:T(8,128)}, u32[]{:S(2)}) copy-start(f32[8,64,128]{1,0,2:T(8,128)} %copy.190) | copy-start | bytes 786436
  1362.2 22.4 %copy-start.4 = (bf16[1,128,2,128]{3,1,2,0:T(8,128)(2,1)S(1)}, bf16[1,128,2,128]{3,1,2,0:T(8,128)(2,1)}, u32[]{:S(2)}) copy-start(bf16[1,128,2,128]{3,1,2,0:T(8,128)(2,1)} %copy-done.3) | copy-start | bytes 196612
  1362.2 22.4 %copy-start.6 = (bf16[1,128,2,128]{3,1,2,0:T(8,128)(2,1)S(1)}, bf16[1,128,2,128]{3,1,2,0:T(8,128)(2,1)}, u32[]{:S(2)}) copy-start(bf16[1,128,2,128]{3,1,2,0:T(8,128)(2,1)} %copy-done.5) | copy-start | bytes 196612
  1389.8 10.8 copy-start.22
  1389.8 10.7 copy-start.25
  1412.6 7.6 copy-start.28
  1412.6 7.7 copy-start.29

commit v2 on v1

--- a/solution.py
+++ b/solution.py
@@ -411,6 +411,312 @@
     )(signal, *operands)
 
 
+def forward_kernel(
+    order_ref, x_ref, cosine_ref, sine_ref, left_ref, right_ref, out_ref, lifted, mixed, spread
+):
+    step = pl.program_id(1)
+    chunk = x_ref.shape[2]
+    outer_size = x_ref.shape[1]
+    tile = x_ref.shape[3]
+    tiles = mixed.shape[0]
+    rows = 2 * outer_size
+    chunks = FACTOR // (2 * chunk)
+
+    @pl.when(step < chunks)
+    def _():
+        lifted[...] = x_ref[0].reshape(outer_size * chunk * tile, FACTOR).astype(jnp.float32)
+        left = left_ref[...]
+
+        def one_column(n, carry):
+            base = n * (tile // 2)
+            parts = []
+            for j in range(tiles):
+                parts.append(
+                    jnp.concatenate(
+                        [
+                            lifted[pl.ds(base + c * tiles + j, outer_size, stride=chunk * tile), :]
+                            for c in range(2)
+                        ],
+                        axis=0,
+                    )
+                )
+            signal = jnp.concatenate(parts, axis=1).astype(jnp.bfloat16)
+            product = jnp.dot(left, signal, preferred_element_type=jnp.float32)
+            cosine, sine = cosine_ref[n], sine_ref[n]
+            start = pl.multiple_of((step * 2 * chunk + n) * rows, rows)
+            for j in range(tiles):
+                lanes = slice(j * FACTOR, (j + 1) * FACTOR)
+                re, im = product[:outer_size, lanes], product[outer_size:, lanes]
+                mixed[j, pl.ds(start, outer_size), :] = re * cosine + im * sine
+                mixed[j, pl.ds(start + outer_size, outer_size), :] = im * cosine - re * sine
+            return carry
+
+        lax.fori_loop(0, 2 * chunk, one_column, 0)
+
+    @pl.when(step >= chunks)
+    def _():
+        right = right_ref[...]
+        j = jnp.maximum(step - chunks, 0)
+
+        def one_row(k, carry):
+            signal = jnp.concatenate(
+                [mixed[j, pl.ds(k + c * outer_size, FACTOR, stride=rows), :] for c in range(2)],
+                axis=0,
+            ).astype(jnp.bfloat16)
+            product = jnp.dot(right, signal, preferred_element_type=jnp.float32)
+            for c in range(2):
+                spread[pl.ds(k + c * outer_size, FACTOR, stride=rows), :] = product[
+                    c * FACTOR : (c + 1) * FACTOR
+                ]
+            return carry
+
+        lax.fori_loop(0, outer_size, one_row, 0)
+        out_ref[0] = spread[...].reshape(FACTOR, rows, FACTOR).astype(jnp.bfloat16)
+
+
+def forward_azimuth(arrived, block_order, tables):
+    blocks, outer_size, pairs, tile, _ = arrived.shape
+    tiles = tile // 4
+    rows = 2 * outer_size
+    chunk = 8
+    chunks = pairs // chunk
+    left = tables[0].reshape(rows, rows)
+    right = tables[1].reshape(2 * FACTOR, 2 * FACTOR).T
+    cosine = jnp.broadcast_to(jnp.cos(tables[2]).T[:, :, None], (FACTOR, outer_size, FACTOR))
+    sine = jnp.broadcast_to(jnp.sin(tables[2]).T[:, :, None], (FACTOR, outer_size, FACTOR))
+    twist = pl.BlockSpec(
+        (2 * chunk, outer_size, FACTOR), lambda b, s, order: (jnp.minimum(s, chunks - 1), 0, 0)
+    )
+    return pl.pallas_call(
+        forward_kernel,
+        grid_spec=pltpu.PrefetchScalarGridSpec(
+            num_scalar_prefetch=1,
+            grid=(blocks, chunks + tiles),
+            in_specs=[
+                pl.BlockSpec(
+                    (1, outer_size, chunk, tile, FACTOR),
+                    lambda b, s, order: (order[b], 0, jnp.minimum(s, chunks - 1), 0, 0),
+                ),
+                twist,
+                twist,
+                pl.BlockSpec(left.shape, lambda b, s, order: (0, 0)),
+                pl.BlockSpec(right.shape, lambda b, s, order: (0, 0)),
+            ],
+            out_specs=pl.BlockSpec(
+                (1, FACTOR, rows, FACTOR),
+                lambda b, s, order: (b, 0, 0, jnp.maximum(s - chunks, 0)),
+            ),
+            scratch_shapes=[
+                pltpu.VMEM((outer_size * chunk * tile, FACTOR), jnp.float32),
+                pltpu.VMEM((tiles, FACTOR * rows, FACTOR), jnp.float32),
+                pltpu.VMEM((FACTOR * rows, FACTOR), jnp.float32),
+            ],
+        ),
+        out_shape=jax.ShapeDtypeStruct((blocks, FACTOR, rows, tiles * FACTOR), jnp.bfloat16),
+        compiler_params=pltpu.CompilerParams(vmem_limit_bytes=44 * 2**20),
+        name="azimuth_forward",
+    )(block_order, arrived, cosine, sine, left, right)
+
+
+def back_kernel(
+    here_ref,
+    before_ref,
+    after_ref,
+    halo_ref,
+    coefficient_ref,
+    offset_ref,
+    spectra_ref,
+    right_ref,
+    left_ref,
+    cosine_ref,
+    sine_ref,
+    out_ref,
+    filtered,
+    turned,
+):
+    tile = pl.program_id(0)
+    step = pl.program_id(1)
+    blocks, groups, rows, _ = here_ref.shape
+    outer_size = rows // 2
+    chunks = FACTOR // groups
+    last = pl.num_programs(0) - 1
+
+    @pl.when(step < chunks)
+    def _():
+        row = lax.broadcasted_iota(jnp.int32, (2 * FACTOR, FACTOR), 0)
+        lane = lax.broadcasted_iota(jnp.int32, (2 * FACTOR, FACTOR), 1)
+        spot = jnp.where(
+            row < FACTOR + BAND_BINS, row, jnp.where(row < 2 * FACTOR, row - 2 * FACTOR, row)
+        )
+        spot = jnp.where(row < FACTOR, row, spot)
+        column = spot + MARGIN_BINS - lane
+        side = lax.broadcasted_iota(jnp.int32, (rows, FACTOR), 1)
+
+        def one_group(g, carry):
+            gap = column - offset_ref[0, pl.ds(g, 1), :]
+            taps = coefficient_ref[0, g]
+            table = jnp.zeros((2 * FACTOR, FACTOR), jnp.float32)
+            for s in range(KERNEL):
+                table = jnp.where(gap == s, taps[s : s + 1, :], table)
+            table = table.astype(jnp.bfloat16)
+            windows = []
+            for b in range(blocks):
+                halo = halo_ref[b, g].astype(jnp.float32)
+                after = jnp.where(tile == last, halo, after_ref[b, g].astype(jnp.float32))
+                before = jnp.where(tile == 0, halo, before_ref[b, g].astype(jnp.float32))
+                edges = jnp.where(side < BAND_BINS, after, before).astype(jnp.bfloat16)
+                windows.append(jnp.concatenate([here_ref[b, g], edges], axis=1))
+            moved = jnp.dot(
+                jnp.concatenate(windows, axis=0), table, preferred_element_type=jnp.float32
+            )
+            spec_real, spec_imag = spectra_ref[0, g, :outer_size], spectra_ref[0, g, outer_size:]
+            start = pl.multiple_of((step * groups + g) * rows, rows)
+            for b in range(blocks):
+                re = moved[b * rows : b * rows + outer_size]
+                im = moved[b * rows + outer_size : (b + 1) * rows]
+                filtered[b, pl.ds(start, outer_size), :] = re * spec_real + im * spec_imag
+                filtered[b, pl.ds(start + outer_size, outer_size), :] = (
+                    im * spec_real - re * spec_imag
+                )
+            return carry
+
+        lax.fori_loop(0, groups, one_group, 0)
+
+    @pl.when(step >= chunks)
+    def _():
+        b = jnp.maximum(step - chunks, 0)
+        right = right_ref[...]
+        left = left_ref[...]
+
+        def one_row(k, carry):
+            signal = jnp.concatenate(
+                [filtered[b, pl.ds(k + c * outer_size, FACTOR, stride=rows), :] for c in range(2)],
+                axis=0,
+            ).astype(jnp.bfloat16)
+            returned = lax.dot_general(
+                signal, right, (((0,), (0,)), ((), ())), preferred_element_type=jnp.float32
+            )
+            cosine, sine = cosine_ref[pl.ds(k, 1), :], sine_ref[pl.ds(k, 1), :]
+            re, im = returned[:, :FACTOR], returned[:, FACTOR:]
+            turned[pl.ds(k, FACTOR, stride=rows), :] = re * cosine - im * sine
+            turned[pl.ds(k + outer_size, FACTOR, stride=rows), :] = re * sine + im * cosine
+            return carry
+
+        lax.fori_loop(0, outer_size, one_row, 0)
+        wide = left.shape[0]
+        each = wide // rows
+
+        def some_bins(r, carry):
+            start = pl.multiple_of(r * wide, wide)
+            signal = turned[pl.ds(start, wide), :].astype(jnp.bfloat16)
+            lines = jnp.dot(left, signal, preferred_element_type=jnp.float32) * (1.0 / PULSES)
+            out_ref[0, pl.ds(r * each, each)] = lines.reshape(each, rows, FACTOR).astype(
+                jnp.bfloat16
+            )
+            return carry
+
+        lax.fori_loop(0, FACTOR // each, some_bins, 0)
+
+
+def back_azimuth(spectral, halo, spectra, coefficients, offsets, tables):
+    blocks, _, rows, width = spectral.shape
+    tiles = width // FACTOR
+    outer_size = rows // 2
+    groups = 8
+    chunks = FACTOR // groups
+    per_tile = FACTOR // BAND_BINS
+    taps = (
+        coefficients.reshape(tiles, per_tile, KERNEL, BAND_BINS, FACTOR)
+        .transpose(0, 4, 2, 1, 3)
+        .reshape(tiles, FACTOR, KERNEL, FACTOR)
+        .astype(jnp.float32)
+    )
+    shifts = jnp.repeat(
+        offsets.reshape(tiles, per_tile, FACTOR).transpose(0, 2, 1), BAND_BINS, axis=2
+    )
+    doppler = jnp.repeat(
+        spectra.reshape(tiles, per_tile, outer_size, 2, FACTOR)
+        .transpose(0, 4, 3, 2, 1)
+        .reshape(tiles, FACTOR, rows, per_tile),
+        BAND_BINS,
+        axis=3,
+    )
+    right = tables[4].reshape(2 * FACTOR, 2 * FACTOR)
+    small = tables[3].transpose(1, 0, 2, 3).reshape(rows, rows)
+    left = jnp.kron(jnp.eye(2 * FACTOR // rows, dtype=jnp.float32), small.astype(jnp.float32))
+    left = left.astype(jnp.bfloat16)
+
+    def at(s):
+        return jnp.minimum(s, chunks - 1)
+
+    def piece(shift):
+        return pl.BlockSpec(
+            (blocks, groups, rows, FACTOR),
+            lambda t, s: (0, at(s), 0, jnp.clip(t + shift, 0, tiles - 1)),
+        )
+
+    def whole(array):
+        return pl.BlockSpec(array.shape, lambda t, s: (0,) * array.ndim)
+
+    cosine, sine = jnp.cos(tables[2]), jnp.sin(tables[2])
+    image = pl.pallas_call(
+        back_kernel,
+        grid=(tiles, chunks + blocks),
+        in_specs=[
+            piece(0),
+            piece(-1),
+            piece(1),
+            pl.BlockSpec((blocks, groups, rows, FACTOR), lambda t, s: (0, at(s), 0, 0)),
+            pl.BlockSpec((1, groups, KERNEL, FACTOR), lambda t, s: (t, at(s), 0, 0)),
+            pl.BlockSpec((1, groups, FACTOR), lambda t, s: (t, at(s), 0)),
+            pl.BlockSpec((1, groups, rows, FACTOR), lambda t, s: (t, at(s), 0, 0)),
+            whole(right),
+            whole(left),
+            whole(cosine),
+            whole(sine),
+        ],
+        out_specs=pl.BlockSpec(
+            (1, FACTOR, rows, FACTOR), lambda t, s: (jnp.maximum(s - chunks, 0), t, 0, 0)
+        ),
+        out_shape=jax.ShapeDtypeStruct((blocks, width, rows, FACTOR), jnp.bfloat16),
+        scratch_shapes=[
+            pltpu.VMEM((blocks, FACTOR * rows, FACTOR), jnp.float32),
+            pltpu.VMEM((FACTOR * rows, FACTOR), jnp.float32),
+        ],
+        compiler_params=pltpu.CompilerParams(vmem_limit_bytes=44 * 2**20),
+        name="azimuth_back",
+    )(
+        spectral,
+        spectral,
+        spectral,
+        halo,
+        taps,
+        shifts,
+        doppler,
+        right,
+        left,
+        cosine,
+        sine,
+    )
+    return (
+        image.reshape(blocks, width, outer_size, 2, FACTOR)
+        .transpose(0, 1, 3, 2, 4)
+        .reshape(blocks, width, 2, outer_size * FACTOR)
+    )
+
+
+def halo_of(spectral):
+    axes = ("section", "band")
+    count = lax.axis_size(axes)
+    up = [(i, i + 1) for i in range(count - 1)]
+    down = [(i + 1, i) for i in range(count - 1)]
+    width = spectral.shape[3]
+    before = lax.ppermute(spectral[..., width - MARGIN_BINS :], axes, up)
+    after = lax.ppermute(spectral[..., :MARGIN_BINS], axes, down)
+    middle = jnp.zeros(spectral.shape[:3] + (FACTOR - 2 * MARGIN_BINS,), spectral.dtype)
+    return jnp.concatenate([after, middle, before], axis=3)
+
+
 def on_device(echoes, replica, azimuth_taps, coefficients, offsets, block_order):
     sections = lax.axis_size("section")
     bands = lax.axis_size("band")
@@ -420,21 +726,22 @@
     pulse_tables = make_tables(PULSES)
     range_spectrum = exact_spectrum(replica[None], RANGE_BINS)[0]
     spectra = exact_spectrum(azimuth_taps, PULSES)
-    band_spectra = jnp.repeat(jnp.transpose(spectra, (1, 2, 3, 0)), BAND_BINS, axis=3)
-    migration_table = build_migration(coefficients, offsets)
     if direct:
         arrived = compress_and_turn(
             echoes, range_spectrum, (("section", sections), ("band", bands))
-        ).reshape(echoes.shape[0], PULSES, 2, RANGE_BINS // count)
+        )
+        spectral = forward_azimuth(arrived, block_order, pulse_tables)
+        return back_azimuth(
+            spectral, halo_of(spectral), spectra, coefficients, offsets, pulse_tables
+        )
+    band_spectra = jnp.repeat(jnp.transpose(spectra, (1, 2, 3, 0)), BAND_BINS, axis=3)
+    migration_table = build_migration(coefficients, offsets)
     images = []
     for position in range(BLOCKS):
-        if direct:
-            turned = lax.dynamic_index_in_dim(arrived, block_order[position], 0, keepdims=False)
-        else:
-            signal = lax.dynamic_index_in_dim(echoes, block_order[position], 0, keepdims=False)
-            compressed = compress_range(signal, range_spectrum, range_tables)
-            turned = corner_turn(compressed[:, None])[:, 0]
-        images.append(focus_azimuth(turned, migration_table, band_spectra, pulse_tables))
+        signal = lax.dynamic_index_in_dim(echoes, block_order[position], 0, keepdims=False)
+        compressed = compress_range(signal, range_spectrum, range_tables)
+        turned = corner_turn(compressed[:, None])
+        images.append(focus_azimuth(turned[:, 0], migration_table, band_spectra, pulse_tables))
     return jnp.stack(images, axis=0)
 
 

time: 1560 us -> 905 us (0.58); the launches traced: 1540 us -> 904 us
  matrix products: 571 us -> 1.57 us
  Pallas kernels: 373 us -> 821 us
  local copies, waits for them, and re-layouts: 445 us -> 65 us
  other arithmetic: 135 us -> 8.43 us
    dot_general x10 -> x0, matrix products: 570 us -> none  [contract(): jnp.einsum(pattern, left_side, right_side, preferred_element_type=jnp.flo...]
    pallas_call x0 -> x2, Pallas kernels: none -> 448 us  [the longest x1 285 us: back_azimuth(): pl.pallas_call(back_kernel, grid=(tiles, chunks + blocks), in_specs=[piec...]
    reshape x5 -> x3, local copies, waits for them, and re-layouts: 121 us -> 16.7 us  [the longest x1 16.4 us: back_azimuth(): jnp.repeat(spectra.reshape(tiles, per_tile, outer_size, 2, FACTOR).transp...]
    another operation x12 -> x4, other arithmetic: 94 us -> 0.7 us
    unnamed x75 -> x12, local copies, waits for them, and re-layouts: 79 us -> 0.83 us
    slice x14 -> x3, local copies, waits for them, and re-layouts: 91.4 us -> 19.2 us  [the longest x2 12.9 us: halo_of(): after = lax.ppermute(spectral[..., :MARGIN_BINS], axes, down)]
    transpose x3 -> x0, local copies, waits for them, and re-layouts: 55.3 us -> none  [the longest x2 55.2 us: contract(): jnp.einsum(pattern, left_side, right_side, preferred_element_type=jnp.flo...]
    another operation x1, local copies, waits for them, and re-layouts: 41.5 us -> 0.14 us  [right_matrix(): return jnp.stack([leading, trailing], axis=0)]
  transfers between devices with their start and end apart: 4 -> 2, of which waited for: 0 -> 0; matrix products, arithmetic and copies ran while one was open for 29% -> 5% of each run, Pallas kernels for 0% -> 0%
where the time goes in v2:
time: 905 us; the launch traced here: 904 us
  Pallas kernels  821 us (91%)
  local copies, waits for them, and re-layouts  65 us (7%)
    pallas_call x1, Pallas kernels, compress_and_turn(): pl.pallas_call(functools.partial(compress_send_kernel, axes), grid=(steps...  373 us
    pallas_call x1, Pallas kernels, back_azimuth(): pl.pallas_call(back_kernel, grid=(tiles, chunks + blocks), in_specs=[piec...  285 us
    pallas_call x1, Pallas kernels, forward_azimuth(): pl.pallas_call(forward_kernel, grid_spec=pltpu.PrefetchScalarGridSpec(num...  163 us
  transfers between devices with their start and end apart: 2, of which 0 were waited for; matrix products, arithmetic and copies ran while one was open for 5% of the time, Pallas kernels for 0%

profile of v2, /device:TPU:24, one launch (start us, length us, event | category | flops | bytes accessed | tf_op | source)
XLA Modules:
  0.0 904.0 jit_solution(11861641848370589080)
XLA Ops:
  0.1 0.3 fusion.53
  0.3 0.1 broadcast_multiply_fusion.2
  0.4 0.3 fusion.54
  0.7 0.3 fusion.51
  1.0 0.3 broadcast_multiply_fusion
  1.2 0.3 fusion.46
  1.5 0.3 fusion.45
  1.8 0.3 negate_convert_fusion
  2.0 0.3 fusion.48
  2.4 0.1 convert_element_type.238.left_ref
  2.5 0.8 pad_bitcast_fusion
  3.5 0.1 maximum_bitcast_fusion.2
  3.7 0.1 copy.64
  4.0 0.4 convolution_bitcast_fusion.2
  4.4 0.1 copy.62
  4.6 0.1 copy.71.left_ref
  4.7 0.3 multiply_subtract_fusion.1
  5.0 0.4 convolution_bitcast_fusion.1
  5.4 0.1 copy.63
  5.5 0.1 copy.72.right_ref
  5.6 373.0 %compress_turn.1.x_ref = bf16[2,32,64,16,128]{4,3,2,1,0:T(8,128)(2,1)} custom-call(bf16[2,128,256,128]{3,2,1,0:T(8,128)(2,1)} %bitcast.144, bf16[256,256]{1,0:T(8,128)(2,1)S(1)} %copy.71.left_ref, bf16[256,256]{1,0:T(8,128)(2,1)S(1)} %copy.72.right_ref, bf16[256,256]{1,0:T(8,128)(2,1)S(1)} %bitcast.131, bf16[256,256]{1,0:T(8,128)(2,1)S(1)} %reshape.448.left_back_ref, ...), custom_call_target="tpu_custom_call" | custom-call | flops 17179869184 | bytes 33554432 | tf_op jit(solution)/shard_map/compress_turn/pallas_call | solution.py:382
  378.6 0.6 broadcast_in_dim.16.sine_ref
  379.2 0.6 broadcast_in_dim.15.cosine_ref
  379.8 163.3 %azimuth_forward.1.here_ref.before_ref.after_ref = bf16[2,128,64,512]{3,2,1,0:T(8,128)(2,1)} custom-call(s32[2]{0:T(128)S(1)} %copy-done, bf16[2,32,64,16,128]{4,3,2,1,0:T(8,128)(2,1)} %compress_turn.1.x_ref, f32[128,32,128]{2,1,0:T(8,128)S(1)} %broadcast_in_dim.15.cosine_ref, f32[128,32,128]{2,1,0:T(8,128)S(1)} %broadcast_in_dim.16.sine_ref, ...), custom_call_target="tpu_custom_call" | custom-call | tf_op jit(solution)/shard_map/azimuth_forward/pallas_call | solution.py:490
  543.2 6.4 fusion.81
  549.6 6.3 copy.75
  555.9 2.0 collective-permute-start.1
  558.0 6.4 copy.74
  564.4 5.6 collective-permute-start
  570.1 0.1 negate_convert_fusion.1
  570.3 0.1 reshape.460
  570.4 0.2 multiply_convert_fusion
  570.6 0.2 convert_element_type.249.left_ref
  570.9 0.2 reshape.466
  571.1 0.1 copy.83.offset_ref
  571.4 0.1 fusion.67
  571.4 0.4 convolution_bitcast_fusion
  571.9 0.4 fusion
  572.3 0.2 copy.80
  572.5 0.2 convert_bitcast_fusion
  572.8 1.5 copy.78
  574.2 2.0 copy.82.coefficient_ref
  576.3 7.2 broadcast_in_dim.19
  583.5 16.4 %copy.84.spectra_ref = f32[4,128,64,128]{3,2,1,0:T(8,128)} copy(f32[4,128,64,128]{1,3,2,0:T(8,128)} %bitcast.133) | data formatting | bytes 33554432 | tf_op jit(solution)/shard_map/reshape | solution.py:637
  600.0 7.3 copy.76
  607.3 7.2 copy.77
  614.5 4.8 pad_maximum_fusion.halo_ref
  619.3 284.6 %azimuth_back.1 = bf16[2,512,64,128]{3,2,1,0:T(8,128)(2,1)} custom-call(bf16[2,128,64,512]{3,2,1,0:T(8,128)(2,1)} %azimuth_forward.1.here_ref.before_ref.after_ref, bf16[2,128,64,512]{3,2,1,0:T(8,128)(2,1)} %azimuth_forward.1.here_ref.before_ref.after_ref, bf16[2,128,64,512]{3,2,1,0:T(8,128)(2,1)} %azimuth_forward.1.here_ref.before_ref.after_ref, ...), custom_call_target="tpu_custom_call" | custom-call | tf_op jit(solution)/shard_map/azimuth_back/pallas_call | solution.py:662
  (39 shorter events, 1.1 us)
Async XLA Ops:
  378.6 1.2 copy-start
  555.9 14.9 %copy-start.2 = (f32[8,2,1024]{2,1,0:T(2,128)S(1)}, f32[8,2,1024]{2,1,0:T(2,128)}, u32[]{:S(2)}) copy-start(f32[8,2,1024]{2,1,0:T(2,128)} %param.8) | copy-start | bytes 196612
  555.9 15.2 %copy-start.3 = (s32[8,128]{1,0:T(8,128)S(1)}, s32[8,128]{1,0:T(8,128)}, u32[]{:S(2)}) copy-start(s32[8,128]{1,0:T(8,128)} %param.10) | copy-start | bytes 12292
  555.9 51.4 %collective-permute-start.1 = (bf16[2,128,64,32]{1,3,2,0:T(8,128)(2,1)}, bf16[2,128,64,32]{1,3,2,0:T(8,128)(2,1)}, u32[]{:S(2)}, u32[]{:S(2)}) collective-permute-start(bf16[2,128,64,32]{1,3,2,0:T(8,128)(2,1)} %copy.75), channel_id=1, source_target_pairs={{0,1},{1,2},{2,3},{3,4},{4,5},{5,6},{6,7},{7,8},{8,9},{9,10},{10,1... | collective-permute-start | bytes 3145736 | tf_op jit(solution)/shard_map/ppermute | solution.py:714
  558.0 14.5 %copy-start.1 = (bf16[8,8,64,128]{3,2,1,0:T(8,128)(2,1)S(1)}, bf16[8,8,64,128]{3,2,1,0:T(8,128)(2,1)}, u32[]{:S(2)}) copy-start(bf16[8,8,64,128]{3,2,1,0:T(8,128)(2,1)} %param.9) | copy-start | bytes 3145732
  564.4 35.6 %collective-permute-start = (bf16[2,128,64,32]{1,3,2,0:T(8,128)(2,1)}, bf16[2,128,64,32]{1,3,2,0:T(8,128)(2,1)}, u32[]{:S(2)}, u32[]{:S(2)}) collective-permute-start(bf16[2,128,64,32]{1,3,2,0:T(8,128)(2,1)} %copy.74), channel_id=1, source_target_pairs={{1,0},{2,1},{3,2},{4,3},{5,4},{6,5},{7,6},{8,7},{9,8},{10,9},{11,1... | collective-permute-start | bytes 3145736 | tf_op jit(solution)/shard_map/ppermute | solution.py:715

commit v3 on v2

--- a/solution.py
+++ b/solution.py
@@ -451,7 +451,7 @@
                 mixed[j, pl.ds(start + outer_size, outer_size), :] = im * cosine - re * sine
             return carry
 
-        lax.fori_loop(0, 2 * chunk, one_column, 0)
+        lax.fori_loop(0, 2 * chunk, one_column, 0, unroll=4)
 
     @pl.when(step >= chunks)
     def _():
@@ -470,7 +470,7 @@
                 ]
             return carry
 
-        lax.fori_loop(0, outer_size, one_row, 0)
+        lax.fori_loop(0, outer_size, one_row, 0, unroll=4)
         out_ref[0] = spread[...].reshape(FACTOR, rows, FACTOR).astype(jnp.bfloat16)
 
 
@@ -543,22 +543,24 @@
 
     @pl.when(step < chunks)
     def _():
-        row = lax.broadcasted_iota(jnp.int32, (2 * FACTOR, FACTOR), 0)
-        lane = lax.broadcasted_iota(jnp.int32, (2 * FACTOR, FACTOR), 1)
-        spot = jnp.where(
-            row < FACTOR + BAND_BINS, row, jnp.where(row < 2 * FACTOR, row - 2 * FACTOR, row)
-        )
-        spot = jnp.where(row < FACTOR, row, spot)
-        column = spot + MARGIN_BINS - lane
+        shape = (FACTOR + 2 * MARGIN_BINS, FACTOR)
+        row = lax.broadcasted_iota(jnp.int32, shape, 0)
+        lane = lax.broadcasted_iota(jnp.int32, shape, 1)
+        kept = FACTOR + MARGIN_BINS
+        spot = jnp.where(row < kept, row, row - shape[0])
+        column = (spot + MARGIN_BINS - lane).astype(jnp.float32).astype(jnp.bfloat16)
+        blank = jnp.zeros((FACTOR - 2 * MARGIN_BINS, FACTOR), jnp.bfloat16)
         side = lax.broadcasted_iota(jnp.int32, (rows, FACTOR), 1)
 
         def one_group(g, carry):
-            gap = column - offset_ref[0, pl.ds(g, 1), :]
+            gap = column - offset_ref[0, pl.ds(g, 1), :].astype(jnp.bfloat16)
             taps = coefficient_ref[0, g]
-            table = jnp.zeros((2 * FACTOR, FACTOR), jnp.float32)
+            table = jnp.zeros(shape, jnp.bfloat16)
             for s in range(KERNEL):
-                table = jnp.where(gap == s, taps[s : s + 1, :], table)
-            table = table.astype(jnp.bfloat16)
+                table = jnp.where(
+                    gap == jnp.bfloat16(s), taps[s : s + 1, :].astype(jnp.bfloat16), table
+                )
+            table = jnp.concatenate([table[:kept], blank, table[kept:]], axis=0)
             windows = []
             for b in range(blocks):
                 halo = halo_ref[b, g].astype(jnp.float32)
@@ -580,7 +582,7 @@
                 )
             return carry
 
-        lax.fori_loop(0, groups, one_group, 0)
+        lax.fori_loop(0, groups, one_group, 0, unroll=4)
 
     @pl.when(step >= chunks)
     def _():
@@ -602,7 +604,7 @@
             turned[pl.ds(k + outer_size, FACTOR, stride=rows), :] = re * sine + im * cosine
             return carry
 
-        lax.fori_loop(0, outer_size, one_row, 0)
+        lax.fori_loop(0, outer_size, one_row, 0, unroll=4)
         wide = left.shape[0]
         each = wide // rows
 
@@ -615,7 +617,7 @@
             )
             return carry
 
-        lax.fori_loop(0, FACTOR // each, some_bins, 0)
+        lax.fori_loop(0, FACTOR // each, some_bins, 0, unroll=4)
 
 
 def back_azimuth(spectral, halo, spectra, coefficients, offsets, tables):
@@ -633,7 +635,7 @@
     )
     shifts = jnp.repeat(
         offsets.reshape(tiles, per_tile, FACTOR).transpose(0, 2, 1), BAND_BINS, axis=2
-    )
+    ).astype(jnp.float32)
     doppler = jnp.repeat(
         spectra.reshape(tiles, per_tile, outer_size, 2, FACTOR)
         .transpose(0, 4, 3, 2, 1)

time: 905 us -> 679 us (0.75)
  Pallas kernels: 821 us -> 594 us
    pallas_call x1, Pallas kernels: 285 us -> 138 us  [back_azimuth(): pl.pallas_call(back_kernel, grid=(tiles, chunks + blocks), in_specs=[piec...]
    pallas_call x1, Pallas kernels: 163 us -> 82.2 us  [forward_azimuth(): pl.pallas_call(forward_kernel, grid_spec=pltpu.PrefetchScalarGridSpec(num...]
  transfers between devices with their start and end apart: 2 -> 2, of which waited for: 0 -> 0; matrix products, arithmetic and copies ran while one was open for 5% -> 6% of each run, Pallas kernels for 0% -> 0%
where the time goes in v3:
time: 679 us; the launch traced here: 677 us
  Pallas kernels  594 us (87%)
  local copies, waits for them, and re-layouts  65 us (10%)
  other arithmetic  8.43 us (1%)
  starting transfers between devices  7.65 us (1%)
    pallas_call x1, Pallas kernels, compress_and_turn(): pl.pallas_call(functools.partial(compress_send_kernel, axes), grid=(steps...  373 us
    pallas_call x1, Pallas kernels, back_azimuth(): pl.pallas_call(back_kernel, grid=(tiles, chunks + blocks), in_specs=[piec...  138 us
    pallas_call x1, Pallas kernels, forward_azimuth(): pl.pallas_call(forward_kernel, grid_spec=pltpu.PrefetchScalarGridSpec(num...  82.2 us
    reshape x1, local copies, waits for them, and re-layouts, back_azimuth(): jnp.repeat(spectra.reshape(tiles, per_tile, outer_size, 2, FACTOR).transp...  16.4 us
  transfers between devices with their start and end apart: 2, of which 0 were waited for; matrix products, arithmetic and copies ran while one was open for 6% of the time, Pallas kernels for 0%

profile of v3, /device:TPU:24, one launch (start us, length us, event | category | flops | bytes accessed | tf_op | source)
XLA Modules:
  0.0 676.7 jit_solution(17565965177397761905)
XLA Ops:
  0.1 0.3 fusion.53
  0.3 0.1 broadcast_multiply_fusion.2
  0.4 0.3 fusion.54
  0.7 0.3 fusion.51
  1.0 0.3 broadcast_multiply_fusion
  1.2 0.3 fusion.46
  1.5 0.3 fusion.45
  1.8 0.3 negate_convert_fusion
  2.0 0.3 fusion.48
  2.4 0.1 convert_element_type.247.left_ref
  2.5 0.8 pad_bitcast_fusion
  3.5 0.1 maximum_bitcast_fusion.2
  3.7 0.1 copy.64
  4.0 0.4 convolution_bitcast_fusion.2
  4.4 0.1 copy.62
  4.6 0.1 copy.71.left_ref
  4.7 0.3 multiply_subtract_fusion.1
  5.0 0.4 convolution_bitcast_fusion.1
  5.4 0.1 copy.63
  5.5 0.1 copy.72.right_ref
  5.6 373.0 %compress_turn.1.x_ref = bf16[2,32,64,16,128]{4,3,2,1,0:T(8,128)(2,1)} custom-call(bf16[2,128,256,128]{3,2,1,0:T(8,128)(2,1)} %bitcast.144, bf16[256,256]{1,0:T(8,128)(2,1)S(1)} %copy.71.left_ref, bf16[256,256]{1,0:T(8,128)(2,1)S(1)} %copy.72.right_ref, bf16[256,256]{1,0:T(8,128)(2,1)S(1)} %bitcast.131, bf16[256,256]{1,0:T(8,128)(2,1)S(1)} %reshape.446.left_back_ref, ...), custom_call_target="tpu_custom_call" | custom-call | flops 17179869184 | bytes 33554432 | tf_op jit(solution)/shard_map/compress_turn/pallas_call | solution.py:382
  378.6 0.6 broadcast_in_dim.16.sine_ref
  379.2 0.6 broadcast_in_dim.15.cosine_ref
  379.8 82.2 %azimuth_forward.1.here_ref.before_ref.after_ref = bf16[2,128,64,512]{3,2,1,0:T(8,128)(2,1)} custom-call(s32[2]{0:T(128)S(1)} %copy-done, bf16[2,32,64,16,128]{4,3,2,1,0:T(8,128)(2,1)} %compress_turn.1.x_ref, f32[128,32,128]{2,1,0:T(8,128)S(1)} %broadcast_in_dim.15.cosine_ref, f32[128,32,128]{2,1,0:T(8,128)S(1)} %broadcast_in_dim.16.sine_ref, ...), custom_call_target="tpu_custom_call" | custom-call | tf_op jit(solution)/shard_map/azimuth_forward/pallas_call | solution.py:490
  462.1 6.4 fusion.81
  468.5 6.3 copy.75
  474.8 2.0 collective-permute-start.1
  476.9 6.4 copy.74
  483.3 5.6 collective-permute-start
  489.0 0.1 negate_convert_fusion.1
  489.2 0.1 reshape.456
  489.3 0.2 multiply_convert_fusion
  489.5 0.2 convert_element_type.262.left_ref
  489.7 0.1 copy.83.offset_ref
  490.0 0.2 reshape.462
  490.3 0.1 fusion.67
  490.4 0.4 convolution_bitcast_fusion
  490.8 0.4 fusion
  491.2 0.2 copy.80
  491.4 0.2 convert_bitcast_fusion
  491.7 1.5 copy.78
  493.2 2.0 copy.82.coefficient_ref
  495.2 7.2 %broadcast_in_dim.19 = f32[4,128,64,2,64]{1,4,3,2,0:T(8,128)} broadcast(f32[4,128,64,2]{1,3,2,0:T(2,128)S(1)} %copy.80), dimensions={0,1,2,3} | broadcast | bytes 17039360 | tf_op jit(solution)/shard_map/broadcast_in_dim | solution.py:639
  502.4 16.4 %copy.84.spectra_ref = f32[4,128,64,128]{3,2,1,0:T(8,128)} copy(f32[4,128,64,128]{1,3,2,0:T(8,128)} %bitcast.133) | data formatting | bytes 33554432 | tf_op jit(solution)/shard_map/reshape | solution.py:639
  518.9 7.3 %copy.76 = bf16[2,128,64,32]{3,2,1,0:T(8,128)(2,1)} copy(bf16[2,128,64,32]{1,3,2,0:T(8,128)(2,1)} %collective-permute-done) | data formatting | bytes 2097152 | tf_op jit(solution)/shard_map/ppermute | solution.py:717
  526.2 7.2 %copy.77 = bf16[2,128,64,32]{3,2,1,0:T(8,128)(2,1)} copy(bf16[2,128,64,32]{1,3,2,0:T(8,128)(2,1)} %collective-permute-done.1) | data formatting | bytes 2097152 | tf_op jit(solution)/shard_map/ppermute | solution.py:716
  533.4 4.8 pad_maximum_fusion.halo_ref
  538.3 138.4 %azimuth_back.1 = bf16[2,512,64,128]{3,2,1,0:T(8,128)(2,1)} custom-call(bf16[2,128,64,512]{3,2,1,0:T(8,128)(2,1)} %azimuth_forward.1.here_ref.before_ref.after_ref, bf16[2,128,64,512]{3,2,1,0:T(8,128)(2,1)} %azimuth_forward.1.here_ref.before_ref.after_ref, bf16[2,128,64,512]{3,2,1,0:T(8,128)(2,1)} %azimuth_forward.1.here_ref.before_ref.after_ref, ...), custom_call_target="tpu_custom_call" | custom-call | tf_op jit(solution)/shard_map/azimuth_back/pallas_call | solution.py:664
  (40 shorter events, 1.1 us)
Async XLA Ops:
  378.6 1.2 copy-start
  474.8 14.6 %copy-start.3 = (s32[8,128]{1,0:T(8,128)S(1)}, s32[8,128]{1,0:T(8,128)}, u32[]{:S(2)}) copy-start(s32[8,128]{1,0:T(8,128)} %param.10) | copy-start | bytes 12292
  474.8 15.0 %copy-start.2 = (f32[8,2,1024]{2,1,0:T(2,128)S(1)}, f32[8,2,1024]{2,1,0:T(2,128)}, u32[]{:S(2)}) copy-start(f32[8,2,1024]{2,1,0:T(2,128)} %param.8) | copy-start | bytes 196612
  474.8 51.4 %collective-permute-start.1 = (bf16[2,128,64,32]{1,3,2,0:T(8,128)(2,1)}, bf16[2,128,64,32]{1,3,2,0:T(8,128)(2,1)}, u32[]{:S(2)}, u32[]{:S(2)}) collective-permute-start(bf16[2,128,64,32]{1,3,2,0:T(8,128)(2,1)} %copy.75), channel_id=1, source_target_pairs={{0,1},{1,2},{2,3},{3,4},{4,5},{5,6},{6,7},{7,8},{8,9},{9,10},{10,1... | collective-permute-start | bytes 3145736 | tf_op jit(solution)/shard_map/ppermute | solution.py:716
  476.9 14.5 %copy-start.1 = (bf16[8,8,64,128]{3,2,1,0:T(8,128)(2,1)S(1)}, bf16[8,8,64,128]{3,2,1,0:T(8,128)(2,1)}, u32[]{:S(2)}) copy-start(bf16[8,8,64,128]{3,2,1,0:T(8,128)(2,1)} %param.9) | copy-start | bytes 3145732
  483.3 35.6 %collective-permute-start = (bf16[2,128,64,32]{1,3,2,0:T(8,128)(2,1)}, bf16[2,128,64,32]{1,3,2,0:T(8,128)(2,1)}, u32[]{:S(2)}, u32[]{:S(2)}) collective-permute-start(bf16[2,128,64,32]{1,3,2,0:T(8,128)(2,1)} %copy.74), channel_id=1, source_target_pairs={{1,0},{2,1},{3,2},{4,3},{5,4},{6,5},{7,6},{8,7},{9,8},{10,9},{11,1... | collective-permute-start | bytes 3145736 | tf_op jit(solution)/shard_map/ppermute | solution.py:717

commit v4 on v3

--- a/solution.py
+++ b/solution.py
@@ -451,7 +451,7 @@
                 mixed[j, pl.ds(start + outer_size, outer_size), :] = im * cosine - re * sine
             return carry
 
-        lax.fori_loop(0, 2 * chunk, one_column, 0, unroll=4)
+        lax.fori_loop(0, 2 * chunk, one_column, 0, unroll=8)
 
     @pl.when(step >= chunks)
     def _():
@@ -470,7 +470,7 @@
                 ]
             return carry
 
-        lax.fori_loop(0, outer_size, one_row, 0, unroll=4)
+        lax.fori_loop(0, outer_size, one_row, 0, unroll=8)
         out_ref[0] = spread[...].reshape(FACTOR, rows, FACTOR).astype(jnp.bfloat16)
 
 
@@ -582,7 +582,7 @@
                 )
             return carry
 
-        lax.fori_loop(0, groups, one_group, 0, unroll=4)
+        lax.fori_loop(0, groups, one_group, 0, unroll=8)
 
     @pl.when(step >= chunks)
     def _():
@@ -604,7 +604,7 @@
             turned[pl.ds(k + outer_size, FACTOR, stride=rows), :] = re * sine + im * cosine
             return carry
 
-        lax.fori_loop(0, outer_size, one_row, 0, unroll=4)
+        lax.fori_loop(0, outer_size, one_row, 0, unroll=8)
         wide = left.shape[0]
         each = wide // rows
 
@@ -617,7 +617,7 @@
             )
             return carry
 
-        lax.fori_loop(0, FACTOR // each, some_bins, 0, unroll=4)
+        lax.fori_loop(0, FACTOR // each, some_bins, 0, unroll=8)
 
 
 def back_azimuth(spectral, halo, spectra, coefficients, offsets, tables):
@@ -636,13 +636,13 @@
     shifts = jnp.repeat(
         offsets.reshape(tiles, per_tile, FACTOR).transpose(0, 2, 1), BAND_BINS, axis=2
     ).astype(jnp.float32)
-    doppler = jnp.repeat(
+    compact = (
         spectra.reshape(tiles, per_tile, outer_size, 2, FACTOR)
-        .transpose(0, 4, 3, 2, 1)
-        .reshape(tiles, FACTOR, rows, per_tile),
-        BAND_BINS,
-        axis=3,
-    )
+        .transpose(1, 0, 4, 3, 2)
+        .reshape(per_tile, tiles, FACTOR, rows, 1)
+    )
+    lane = lax.broadcasted_iota(jnp.int32, (tiles, FACTOR, rows, FACTOR), 3)
+    doppler = jnp.where(lane < BAND_BINS, compact[0], compact[1])
     right = tables[4].reshape(2 * FACTOR, 2 * FACTOR)
     small = tables[3].transpose(1, 0, 2, 3).reshape(rows, rows)
     left = jnp.kron(jnp.eye(2 * FACTOR // rows, dtype=jnp.float32), small.astype(jnp.float32))

time: 679 us -> 647 us (0.953)
  local copies, waits for them, and re-layouts: 65 us -> 41.4 us
  Pallas kernels: 594 us -> 575 us
  other arithmetic: 8.43 us -> 19.5 us
    reshape x2 -> x1, local copies, waits for them, and re-layouts: 16.6 us -> 0.02 us  [back_azimuth(): spectra.reshape(tiles, per_tile, outer_size, 2, FACTOR)]
    pallas_call x1, Pallas kernels: 138 us -> 125 us  [back_azimuth(): pl.pallas_call(back_kernel, grid=(tiles, chunks + blocks), in_specs=[piec...]
    select_n x0 -> x1, other arithmetic: none -> 11 us  [back_azimuth(): doppler = jnp.where(lane < BAND_BINS, compact[0], compact[1])]
    broadcast_in_dim x1 -> x2, local copies, waits for them, and re-layouts: 7.24 us -> 0.26 us  [back_azimuth(): doppler = jnp.where(lane < BAND_BINS, compact[0], compact[1])]
  transfers between devices with their start and end apart: 2 -> 2, of which waited for: 0 -> 0; matrix products, arithmetic and copies ran while one was open for 6% -> 5% of each run, Pallas kernels for 0% -> 0%
where the time goes in v4:
time: 647 us; the launch traced here: 646 us
  Pallas kernels  575 us (89%)
  local copies, waits for them, and re-layouts  41.4 us (6%)
  other arithmetic  19.5 us (3%)
  starting transfers between devices  7.78 us (1%)
    pallas_call x1, Pallas kernels, compress_and_turn(): pl.pallas_call(functools.partial(compress_send_kernel, axes), grid=(steps...  373 us
    pallas_call x1, Pallas kernels, back_azimuth(): pl.pallas_call(back_kernel, grid=(tiles, chunks + blocks), in_specs=[piec...  125 us
    pallas_call x1, Pallas kernels, forward_azimuth(): pl.pallas_call(forward_kernel, grid_spec=pltpu.PrefetchScalarGridSpec(num...  77.3 us
  transfers between devices with their start and end apart: 2, of which 0 were waited for; matrix products, arithmetic and copies ran while one was open for 5% of the time, Pallas kernels for 0%

profile of v4, /device:TPU:24, one launch (start us, length us, event | category | flops | bytes accessed | tf_op | source)
XLA Modules:
  0.0 645.6 jit_solution(15057258229269156092)
XLA Ops:
  0.1 0.3 fusion.53
  0.3 0.1 broadcast_multiply_fusion.2
  0.4 0.3 fusion.54
  0.7 0.3 fusion.51
  1.0 0.3 broadcast_multiply_fusion
  1.2 0.3 fusion.46
  1.5 0.3 fusion.45
  1.8 0.3 negate_convert_fusion
  2.0 0.3 fusion.48
  2.4 0.1 convert_element_type.247.left_ref
  2.5 0.8 pad_bitcast_fusion
  3.5 0.1 maximum_bitcast_fusion.2
  3.7 0.1 copy.67
  4.0 0.4 convolution_bitcast_fusion.2
  4.4 0.1 copy.65
  4.6 0.1 copy.74.left_ref
  4.7 0.3 multiply_subtract_fusion.1
  5.0 0.4 convolution_bitcast_fusion.1
  5.4 0.1 copy.66
  5.5 0.1 copy.75.right_ref
  5.6 373.0 %compress_turn.1.x_ref = bf16[2,32,64,16,128]{4,3,2,1,0:T(8,128)(2,1)} custom-call(bf16[2,128,256,128]{3,2,1,0:T(8,128)(2,1)} %bitcast.146, bf16[256,256]{1,0:T(8,128)(2,1)S(1)} %copy.74.left_ref, bf16[256,256]{1,0:T(8,128)(2,1)S(1)} %copy.75.right_ref, bf16[256,256]{1,0:T(8,128)(2,1)S(1)} %bitcast.131, bf16[256,256]{1,0:T(8,128)(2,1)S(1)} %reshape.447.left_back_ref, ...), custom_call_target="tpu_custom_call" | custom-call | flops 17179869184 | bytes 33554432 | tf_op jit(solution)/shard_map/compress_turn/pallas_call | solution.py:382
  378.6 0.6 broadcast_in_dim.28.sine_ref
  379.2 0.6 broadcast_in_dim.27.cosine_ref
  379.8 77.3 %azimuth_forward.1.here_ref.before_ref.after_ref = bf16[2,128,64,512]{3,2,1,0:T(8,128)(2,1)} custom-call(s32[2]{0:T(128)S(1)} %copy-done, bf16[2,32,64,16,128]{4,3,2,1,0:T(8,128)(2,1)} %compress_turn.1.x_ref, f32[128,32,128]{2,1,0:T(8,128)S(1)} %broadcast_in_dim.27.cosine_ref, f32[128,32,128]{2,1,0:T(8,128)S(1)} %broadcast_in_dim.28.sine_ref, ...), custom_call_target="tpu_custom_call" | custom-call | tf_op jit(solution)/shard_map/azimuth_forward/pallas_call | solution.py:490
  457.1 6.4 fusion.81
  463.5 6.3 copy.78
  469.9 2.0 collective-permute-start.1
  471.9 6.3 copy.77
  478.3 5.7 collective-permute-start
  484.2 0.1 negate_convert_fusion.1
  484.3 0.1 fusion.67
  484.5 0.1 reshape.455
  484.6 0.2 multiply_convert_fusion
  484.8 0.2 convert_element_type.262.left_ref
  485.0 0.1 copy.88.offset_ref
  485.2 0.2 reshape.461
  485.5 0.4 convolution_bitcast_fusion
  485.9 0.4 fusion
  486.4 0.1 copy.85
  486.5 0.1 copy.84
  486.6 0.2 convert_bitcast_fusion
  486.9 1.5 copy.81
  488.4 2.0 copy.87.coefficient_ref
  490.5 11.0 %broadcast_select_fusion.spectra_ref = f32[4,128,64,128]{3,2,1,0:T(8,128)} fusion(f32[4,128,64]{2,1,0:T(8,128)S(1)} %copy.85, f32[4,128,64]{2,1,0:T(8,128)S(1)} %copy.84, pred[128]{0:T(512)(128)(4,1)S(1)} %iota_compare_fusion.1), kind=kLoop, calls=%fused_computation | loop fusion | flops 4194304 | bytes 17039488 | tf_op jit(solution)/shard_map/jit(_where)/select_n | solution.py:645
  501.5 7.3 %copy.79 = bf16[2,128,64,32]{3,2,1,0:T(8,128)(2,1)} copy(bf16[2,128,64,32]{1,3,2,0:T(8,128)(2,1)} %collective-permute-done) | data formatting | bytes 2097152 | tf_op jit(solution)/shard_map/ppermute | solution.py:717
  508.8 7.2 %copy.80 = bf16[2,128,64,32]{3,2,1,0:T(8,128)(2,1)} copy(bf16[2,128,64,32]{1,3,2,0:T(8,128)(2,1)} %collective-permute-done.1) | data formatting | bytes 2097152 | tf_op jit(solution)/shard_map/ppermute | solution.py:716
  516.0 4.8 pad_maximum_fusion.halo_ref
  520.9 124.7 %azimuth_back.1 = bf16[2,512,64,128]{3,2,1,0:T(8,128)(2,1)} custom-call(bf16[2,128,64,512]{3,2,1,0:T(8,128)(2,1)} %azimuth_forward.1.here_ref.before_ref.after_ref, bf16[2,128,64,512]{3,2,1,0:T(8,128)(2,1)} %azimuth_forward.1.here_ref.before_ref.after_ref, bf16[2,128,64,512]{3,2,1,0:T(8,128)(2,1)} %azimuth_forward.1.here_ref.before_ref.after_ref, ...), custom_call_target="tpu_custom_call" | custom-call | tf_op jit(solution)/shard_map/azimuth_back/pallas_call | solution.py:664
  (43 shorter events, 1.2 us)
Async XLA Ops:
  378.6 1.2 copy-start
  463.5 20.8 %copy-start.3 = (s32[8,128]{1,0:T(8,128)S(1)}, s32[8,128]{1,0:T(8,128)}, u32[]{:S(2)}) copy-start(s32[8,128]{1,0:T(8,128)} %param.10) | copy-start | bytes 12292
  469.9 15.3 %copy-start.2 = (f32[8,2,1024]{2,1,0:T(2,128)S(1)}, f32[8,2,1024]{2,1,0:T(2,128)}, u32[]{:S(2)}) copy-start(f32[8,2,1024]{2,1,0:T(2,128)} %param.8) | copy-start | bytes 196612
  469.9 39.0 %collective-permute-start.1 = (bf16[2,128,64,32]{1,3,2,0:T(8,128)(2,1)}, bf16[2,128,64,32]{1,3,2,0:T(8,128)(2,1)}, u32[]{:S(2)}, u32[]{:S(2)}) collective-permute-start(bf16[2,128,64,32]{1,3,2,0:T(8,128)(2,1)} %copy.78), channel_id=1, source_target_pairs={{0,1},{1,2},{2,3},{3,4},{4,5},{5,6},{6,7},{7,8},{8,9},{9,10},{10,1... | collective-permute-start | bytes 3145736 | tf_op jit(solution)/shard_map/ppermute | solution.py:716
  478.3 8.4 %copy-start.1 = (bf16[8,8,64,128]{3,2,1,0:T(8,128)(2,1)S(1)}, bf16[8,8,64,128]{3,2,1,0:T(8,128)(2,1)}, u32[]{:S(2)}) copy-start(bf16[8,8,64,128]{3,2,1,0:T(8,128)(2,1)} %param.9) | copy-start | bytes 3145732
  478.3 23.2 %collective-permute-start = (bf16[2,128,64,32]{1,3,2,0:T(8,128)(2,1)}, bf16[2,128,64,32]{1,3,2,0:T(8,128)(2,1)}, u32[]{:S(2)}, u32[]{:S(2)}) collective-permute-start(bf16[2,128,64,32]{1,3,2,0:T(8,128)(2,1)} %copy.77), channel_id=1, source_target_pairs={{1,0},{2,1},{3,2},{4,3},{5,4},{6,5},{7,6},{8,7},{9,8},{10,9},{11,1... | collective-permute-start | bytes 3145736 | tf_op jit(solution)/shard_map/ppermute | solution.py:717
